TPU v7x, 32 devices: a whole 2x2x4 slice. The times are simulated.
32 devices in a mesh: dp: 8 (over z, x), blk: 4 (over y, core).
Axes of the slice: x: 2, y: 2, z: 4, core: 2. Of those that a mesh axis runs over, the one named last changes fastest.
Arguments:
- patches: bfloat16 [8, 1024, 1024], P('dp', 'blk'), may hold values from -6 to 6
- cotangent: bfloat16 [8, 1024, 1024], P('dp', 'blk'), may hold values from -6 to 6
- image_lengths: int32 [8, 9], P('dp'), may hold values from 1 to 770, as said below
- params: float32 [12595200], P(('dp', 'blk')), may hold values from -1.5 to 1.75
- first_moment: float32 [12595200], P(('dp', 'blk')), may hold values from -0.0006 to 0.0006
- second_moment: float32 [12595200], P(('dp', 'blk')), may hold values from 1e-09 to 1e-07
Outputs:
- activations: bfloat16 [8, 1024, 1024], P('dp', 'blk')
- input_grad: bfloat16 [8, 1024, 1024], P('dp', 'blk')
- norms: float32 [12], replicated
- param_step: float32 [12595200], P(('dp', 'blk'))
- new_first: float32 [12595200], P(('dp', 'blk'))
- down_bias_grad: float32 [1024], replicated
Inputs may be any that keep to these rules, and one draw needn't show every extreme that they name: `image_lengths`: each row holds the patch counts of 8 images of one packed sequence and then its padding count; a row sums to 1024; in each row exactly one image has 770 patches.
All inputs are finite; a program needn't handle non-finite values.
Results may differ from a plain program's by a relative error of at most 0.014.
Values may be sent and summed in bfloat16 or wider, within the bound.
A program may use at most 256 MiB of HBM per device.

v0:
```python
from functools import partial
import math

import jax
import jax.numpy as jnp
from jax import lax
from jax.sharding import PartitionSpec as P

D = 1024
FF = 4096
HEADS = 16
HEAD_DIM = 64
GROUPS = 12
RAW = 12595200


eps_norm = 1e-06
neg_big = -1e30


def starts_of(model_width, hidden):
    square = model_width * model_width
    mlp_start = 7 * model_width + 4 * square
    return [
        0,
        model_width,
        2 * model_width,
        2 * model_width + 3 * square,
        4 * model_width + 3 * square,
        4 * model_width + 4 * square,
        5 * model_width + 4 * square,
        6 * model_width + 4 * square,
        mlp_start,
        mlp_start + model_width * hidden,
        mlp_start + model_width * hidden + hidden,
        mlp_start + 2 * model_width * hidden + hidden,
        mlp_start + 2 * model_width * hidden + hidden + model_width,
    ]


def unpack(flat_params):
    marks = starts_of(D, FF)
    pieces = [flat_params[marks[member] : marks[member + 1]] for member in range(12)]
    return (
        pieces[0],
        pieces[1],
        pieces[2].reshape(D, 3 * D),
        pieces[3],
        pieces[4].reshape(D, D),
        pieces[5],
        pieces[6],
        pieces[7],
        pieces[8].reshape(D, FF),
        pieces[9],
        pieces[10].reshape(FF, D),
        pieces[11],
    )


def layer_norm(values, gains, offsets):
    average = jnp.mean(values, axis=-1, keepdims=True)
    centred = values - average
    spread = jnp.mean(centred * centred, axis=-1, keepdims=True)
    return centred * lax.rsqrt(spread + eps_norm) * gains + offsets


def segment_ids(lengths, row_ids):
    bounds = jnp.cumsum(lengths)
    return jnp.sum((row_ids[:, None] >= bounds[None, :]).astype(jnp.int32), axis=1)


def shards(patches, cotangent, image_lengths, params, first_moment, second_moment):
    local_rows = patches.shape[1]
    seq_len = local_rows * lax.axis_size("blk")
    scale_of = HEAD_DIM ** (-0.5)
    inputs = patches[0].astype(jnp.float32)
    lengths = image_lengths[0]
    query_ids = lax.axis_index("blk") * local_rows + jnp.arange(local_rows, dtype=jnp.int32)
    query_labels = segment_ids(lengths, query_ids)
    weights_low = lax.all_gather(params.astype(jnp.bfloat16), ("dp", "blk"), axis=0, tiled=True)
    (
        gain_one,
        shift_one,
        w_qkv,
        bias_qv,
        w_out,
        bias_out,
        gain_two,
        shift_two,
        w_up,
        bias_up,
        w_down,
        bias_down,
    ) = unpack(weights_low)
    normed_one, pull_one = jax.vjp(
        layer_norm, inputs, gain_one.astype(jnp.float32), shift_one.astype(jnp.float32)
    )
    normed_low = normed_one.astype(jnp.bfloat16)
    bias_all = jnp.concatenate(
        [
            bias_qv[:D].astype(jnp.float32),
            jnp.zeros((D,), jnp.float32),
            bias_qv[D:].astype(jnp.float32),
        ]
    )
    projected = (jnp.dot(normed_low, w_qkv, preferred_element_type=jnp.float32) + bias_all).astype(
        jnp.bfloat16
    )
    queries = projected[:, :D].reshape(local_rows, HEADS, HEAD_DIM)
    key_value = projected[:, D:]

    def attend_block(state, block, block_labels):
        allowed = query_labels[:, None] == block_labels[None, :]
        best_in, total_in, summed_in = state
        raw = jnp.einsum("qhd,khd->hqk", queries, block[:, 0], preferred_element_type=jnp.float32)
        scores = jnp.where(allowed[None], raw * scale_of, neg_big)
        new_best = jnp.maximum(best_in, jnp.max(scores, axis=-1))
        factor = jnp.exp(best_in - new_best)
        weights = jnp.where(allowed[None], jnp.exp(scores - new_best[..., None]), 0.0)
        new_total = total_in * factor + jnp.sum(weights, axis=-1)
        added = jnp.einsum(
            "hqk,khd->qhd",
            weights.astype(jnp.bfloat16),
            block[:, 1],
            preferred_element_type=jnp.float32,
        )
        return (new_best, new_total, summed_in * factor.T[..., None] + added)

    start_state = (
        jnp.full((HEADS, local_rows), neg_big, jnp.float32),
        jnp.zeros((HEADS, local_rows), jnp.float32),
        jnp.zeros((local_rows, HEADS, HEAD_DIM), jnp.float32),
    )
    carry = start_state
    piece = lax.all_gather(key_value, "blk", axis=0, tiled=True)
    count = piece.shape[0]
    size = math.gcd(count, 512)
    blocks = piece.reshape(count // size, size, 2, HEADS, HEAD_DIM)
    labels = segment_ids(lengths, jnp.arange(count, dtype=jnp.int32)).reshape(count // size, size)

    def one_block(state, members):
        return (attend_block(state, members[0], members[1]), None)

    carry, ignored = lax.scan(one_block, carry, (blocks, labels))
    best, total, summed = carry
    attended = summed / total.T[..., None]
    log_total = best + jnp.log(total)
    attended_low = attended.reshape(local_rows, D).astype(jnp.bfloat16)
    branch = jnp.dot(attended_low, w_out, preferred_element_type=jnp.float32) + bias_out.astype(
        jnp.float32
    )
    middle = inputs + branch
    normed_two, pull_two = jax.vjp(
        layer_norm, middle, gain_two.astype(jnp.float32), shift_two.astype(jnp.float32)
    )
    normed_two_low = normed_two.astype(jnp.bfloat16)
    hidden_pre = jnp.dot(normed_two_low, w_up, preferred_element_type=jnp.float32) + bias_up.astype(
        jnp.float32
    )
    activated, pull_gelu = jax.vjp(partial(jax.nn.gelu, approximate=False), hidden_pre)
    activated_low = activated.astype(jnp.bfloat16)
    result = middle + (
        jnp.dot(activated_low, w_down, preferred_element_type=jnp.float32)
        + bias_down.astype(jnp.float32)
    )
    grad_out = cotangent[0]
    grad_down = jnp.dot(activated_low.T, grad_out, preferred_element_type=jnp.float32)
    grad_bias_down = jnp.sum(grad_out.astype(jnp.float32), axis=0)
    grad_act = jnp.dot(grad_out, w_down.T, preferred_element_type=jnp.float32)
    grad_hidden_low = pull_gelu(grad_act)[0].astype(jnp.bfloat16)
    grad_up = jnp.dot(normed_two_low.T, grad_hidden_low, preferred_element_type=jnp.float32)
    grad_bias_up = jnp.sum(grad_hidden_low.astype(jnp.float32), axis=0)
    grad_normed_two = jnp.dot(grad_hidden_low, w_up.T, preferred_element_type=jnp.float32)
    grad_mid_norm, grad_gain_two, grad_shift_two = pull_two(grad_normed_two)
    grad_middle = grad_out.astype(jnp.float32) + grad_mid_norm
    grad_middle_low = grad_middle.astype(jnp.bfloat16)
    grad_w_out = jnp.dot(attended_low.T, grad_middle_low, preferred_element_type=jnp.float32)
    grad_bias_out = jnp.sum(grad_middle_low.astype(jnp.float32), axis=0)
    grad_attended = (
        jnp.dot(grad_middle_low, w_out.T, preferred_element_type=jnp.float32)
        .astype(jnp.bfloat16)
        .reshape(local_rows, HEADS, HEAD_DIM)
    )
    delta_rows = jnp.sum(grad_attended.astype(jnp.float32) * attended, axis=-1).T
    gathered = lax.all_gather(key_value, "blk", axis=0, tiled=True)
    size = math.gcd(seq_len, 512)
    key_blocks = gathered.reshape(seq_len // size, size, 2, HEADS, HEAD_DIM)
    key_labels = segment_ids(lengths, jnp.arange(seq_len, dtype=jnp.int32)).reshape(
        seq_len // size, size
    )

    def back_block(grad_query, members):
        block, block_labels = members
        allowed = query_labels[:, None] == block_labels[None, :]
        raw = jnp.einsum("qhd,khd->hqk", queries, block[:, 0], preferred_element_type=jnp.float32)
        scores = jnp.where(allowed[None], raw * scale_of, neg_big)
        probs = jnp.where(allowed[None], jnp.exp(scores - log_total[..., None]), 0.0)
        grad_probs = jnp.einsum(
            "qhd,khd->hqk", grad_attended, block[:, 1], preferred_element_type=jnp.float32
        )
        grad_raw = (probs * (grad_probs - delta_rows[..., None]) * scale_of).astype(jnp.bfloat16)
        new_grad = grad_query + jnp.einsum(
            "hqk,khd->qhd", grad_raw, block[:, 0], preferred_element_type=jnp.float32
        )
        grad_keys = jnp.einsum(
            "hqk,qhd->khd", grad_raw, queries, preferred_element_type=jnp.float32
        )
        grad_values = jnp.einsum(
            "hqk,qhd->khd",
            probs.astype(jnp.bfloat16),
            grad_attended,
            preferred_element_type=jnp.float32,
        )
        return (new_grad, jnp.stack([grad_keys, grad_values], axis=1))

    grad_query, grad_kv_blocks = lax.scan(
        back_block, jnp.zeros((local_rows, HEADS, HEAD_DIM), jnp.float32), (key_blocks, key_labels)
    )
    grad_kv = lax.psum_scatter(
        grad_kv_blocks.reshape(seq_len, 2 * D).astype(jnp.bfloat16),
        "blk",
        scatter_dimension=0,
        tiled=True,
    ).astype(jnp.float32)
    grad_projected = jnp.concatenate([grad_query.reshape(local_rows, D), grad_kv], axis=1).astype(
        jnp.bfloat16
    )
    grad_w_qkv = jnp.dot(normed_low.T, grad_projected, preferred_element_type=jnp.float32)
    grad_proj_rows = jnp.sum(grad_projected.astype(jnp.float32), axis=0)
    grad_bias_qv = jnp.concatenate([grad_proj_rows[:D], grad_proj_rows[2 * D :]])
    grad_normed_one = jnp.dot(grad_projected, w_qkv.T, preferred_element_type=jnp.float32)
    grad_in_norm, grad_gain_one, grad_shift_one = pull_one(grad_normed_one)
    grad_inputs = grad_middle + grad_in_norm
    shard_len = params.shape[0]
    total_params = shard_len * lax.axis_size(("dp", "blk"))
    flat_grad = jnp.concatenate(
        [
            grad_gain_one,
            grad_shift_one,
            grad_w_qkv.reshape(-1),
            grad_bias_qv,
            grad_w_out.reshape(-1),
            grad_bias_out,
            grad_gain_two,
            grad_shift_two,
            grad_up.reshape(-1),
            grad_bias_up,
            grad_down.reshape(-1),
            grad_bias_down,
            jnp.zeros((total_params - RAW,), jnp.float32),
        ]
    )
    shard_grad = lax.psum_scatter(
        lax.slice_in_dim(flat_grad, 0, lax.axis_size(("dp", "blk")) * shard_len, axis=0),
        ("dp", "blk"),
        scatter_dimension=0,
        tiled=True,
    )
    positions = lax.axis_index(("dp", "blk")) * shard_len + jnp.arange(shard_len, dtype=jnp.int32)
    marks = jnp.array(starts_of(D, FF), dtype=jnp.int32)
    group_of = jnp.sum((positions[:, None] >= marks[None, :]).astype(jnp.int32), axis=1) - 1
    squares = shard_grad * shard_grad
    partials = jnp.sum(
        jnp.where(
            group_of[None, :] == jnp.arange(GROUPS, dtype=jnp.int32)[:, None], squares[None, :], 0.0
        ),
        axis=1,
    )
    norms, bias_total = lax.psum((partials, grad_bias_down), ("dp", "blk"))
    clip_factor = 1.0 / jnp.maximum(jnp.sqrt(jnp.sum(norms)), 1.0)
    decayed = ((group_of == 2) | (group_of == 4) | (group_of == 8) | (group_of == 10)).astype(
        jnp.float32
    )
    scaled = clip_factor * shard_grad
    new_first = 0.9 * first_moment + 0.1 * scaled
    new_second = 0.999 * second_moment + 0.001 * scaled * scaled
    direction = new_first / (1.0 - 0.9**10) / (jnp.sqrt(new_second / (1.0 - 0.999**10)) + 1e-08)
    param_step = -0.001 * 0.9**12 * (direction + 0.05 * decayed * params)
    return (
        result.astype(jnp.bfloat16)[None],
        grad_inputs.astype(jnp.bfloat16)[None],
        norms,
        param_step,
        new_first,
        bias_total,
    )


def solution(mesh):
    in_specs = (
        P("dp", "blk", None),
        P("dp", "blk", None),
        P("dp", None),
        P(("dp", "blk")),
        P(("dp", "blk")),
        P(("dp", "blk")),
    )
    out_specs = (
        P("dp", "blk", None),
        P("dp", "blk", None),
        P(),
        P(("dp", "blk")),
        P(("dp", "blk")),
        P(),
    )
    return jax.shard_map(shards, mesh=mesh, in_specs=in_specs, out_specs=out_specs, check_vma=False)
```

profile of v0, /device:TPU:0, one launch (start us, length us, event | category | flops | bytes accessed | tf_op | source)
XLA Modules:
  0.0 1632.5 jit_solution(10347074560292992285)
XLA Ops:
  7.2 1.5 convert_element_type.123
  8.8 9.7 reshape.277
  19.5 277.6 %all-gather.6.cloned.1.call-done = bf16[32,1,393600]{2,1,0:T(2,128)(2,1)} async-done(((bf16[1,1,393600]{2,1,0:T(2,128)(2,1)}), bf16[32,1,393600]{2,1,0:T(2,128)(2,1)}) %all-gather.6.cloned.1.call-update) | async-done | bytes 25190416 | tf_op jit(solution)/shard_map/all_gather | solution.py:80
  297.1 149.2 %reduce.1 = bf16[32,393600]{1,0:T(8,128)(2,1)} reduce(bf16[32,1,393600]{2,1,0:T(2,128)(2,1)} %all-gather.6.cloned.1.call-done, bf16[]{:T(256)} %constant.178), dimensions={1}, to_apply=%all-gather.reduce_sub_computation | reduce | bytes 50380800 | tf_op jit(solution)/shard_map/all_gather | solution.py:80
  446.3 59.0 %reshape.278 = bf16[12595200]{0:T(1024)(128)(2,1)} reshape(bf16[32,393600]{1,0:T(8,128)(2,1)} %reduce.1) | data formatting | bytes 50380800
  506.6 6.4 slice.116
  513.0 10.4 reshape.267
  523.5 4.7 fusion.42
  530.6 12.0 fusion.99
  542.7 2.0 slice.120
  545.9 2.3 slice.95
  548.3 13.4 reshape.270
  561.6 13.3 slice.102
  575.6 12.9 reshape.279
  588.5 9.8 copy.50
  598.3 32.4 %while.28 = (s32[]{:T(128)}, f32[16,256]{1,0:T(8,128)S(1)}, f32[16,256]{1,0:T(8,128)S(1)}, f32[256,16,64]{0,2,1:T(8,128)}, s32[256]{0:T(256)S(1)}, /*index=5*/s3...) while((s32[]{:T(128)}, f32[16,256]{1,0:T(8,128)S(1)}, ...), condition=%wide.region_8.9_spmd.clone, body=%wide.region_5.8_spmd.clone.sunk | while | flops 565075968 | bytes 68426912 | solution.py:144
  598.4 1.8 dynamic-slice_bitcast_fusion.4
  600.2 4.7 fusion.145
  604.9 4.6 fusion.147
  610.8 3.1 fusion.149
  614.0 1.8 dynamic-slice_bitcast_fusion.4
  615.8 4.7 fusion.145
  620.5 4.6 fusion.147
  626.3 4.4 fusion.149
  632.0 2.6 fusion.100
  635.0 16.7 %multiply_convert_fusion = (bf16[256,4096]{1,0:T(8,128)(2,1)}, f32[256,4096]{1,0:T(8,128)}, f32[256,4096]{1,0:T(8,128)}) fusion(f32[4096]{0:T(1024)S(1)} %slice_convert_fusion, bf16[1024,4096]{1,0:T(8,128)(2,1)} %reshape.270, f32[256,1024]{1,0:T(8,128)S(1)} %get-tuple-element.310, f32[1024]{0:T(1024)S(1)} %get-tuple-element.298, ...), kind=kOutput, calls=%fused_computation.60 | convolution fusion | flops 2218000384 | bytes 19949568 | tf_op jit(solution)/shard_map/dot_general | solution.py:157
  651.7 6.9 convert_reduce_fusion.1
  658.7 7.4 multiply_reduce_fusion
  670.2 49.3 %while.29 = (s32[]{:T(128)}, f32[256,16,64]{0,2,1:T(8,128)}, bf16[2,512,2,16,64]{1,4,3,2,0:T(8,128)(2,1)}, bf16[2,512,2,16,64]{1,4,3,2,0:T(8,128)(2,1)}, s32[256...) while((s32[]{:T(128)}, f32[256,16,64]{0,2,1:T(8,128)}, ...), condition=%wide.region_15.16_spmd.clone, body=%wide.region_14.15_spmd.clone.sunk | while | flops 1374289920 | bytes 144104784 | solution.py:216
  671.2 1.8 dynamic-slice_bitcast_fusion.5
  674.5 6.2 fusion.158
  680.7 3.9 fusion.159
  684.6 5.8 fusion.160
  690.4 1.4 convolution_bitcast_fusion.7
  692.9 2.0 copy-done.17
  695.6 1.8 dynamic-slice_bitcast_fusion.5
  698.9 6.2 fusion.158
  705.1 4.3 fusion.159
  709.4 5.8 fusion.160
  715.1 1.4 convolution_bitcast_fusion.7
  717.6 2.0 copy-done.17
  719.6 6.5 copy.53
  726.1 3.2 copy.60
  731.5 3.0 copy.62
  734.5 2.5 convolution_bitcast_fusion.3
  737.1 7.0 copy.63
  744.1 2.4 convolution_bitcast_fusion.2
  746.5 8.4 copy.64
  754.9 17.3 %reduce-scatter.2.cloned.1.call-done = bf16[256,2048]{0,1:T(8,128)(2,1)} async-done(((bf16[1024,2048]{0,1:T(8,128)(2,1)}), bf16[256,2048]{0,1:T(8,128)(2,1)}) %reduce-scatter.2.cloned.1.call-update) | async-done | bytes 1048592 | tf_op jit(solution)/shard_map/reduce_scatter | solution.py:219
  772.2 5.2 fusion.95
  778.0 1.4 convert_reduce_fusion.4
  780.0 6.6 convolution_bitcast_fusion.4
  786.6 12.1 copy.61
  799.3 11.2 constant_dynamic-update-slice_fusion.8
  812.1 2.4 constant_dynamic-update-slice_fusion.7
  817.1 8.4 constant_dynamic-update-slice_fusion.3
  828.6 6.0 constant_dynamic-update-slice_fusion.1
  835.8 24.4 %convert_reduce_fusion = s32[393600]{0:T(1024)S(1)} fusion(s32[393600]{0:T(1024)S(1)} %iota_add_fusion, s32[13]{0:T(128)S(1)} %copy-done.44), kind=kLoop, calls=%fused_computation.51 | loop fusion | flops 14956800 | bytes 3148852 | tf_op jit(solution)/shard_map/reduce_sum | solution.py:261
  861.5 695.8 %all-reduce.4.cloned.1.call-done = f32[12595200]{0:T(1024)} async-done(((f32[12595200]{0:T(1024)}), f32[12595200]{0:T(1024)}) %all-reduce.4.cloned.1.call-update) | async-done | bytes 50380816
  1557.2 2.0 dynamic-slice_multiply_fusion
  1559.3 12.3 select_reduce_fusion
  1571.6 6.6 fusion.58
  1578.1 40.0 %all-reduce.1 = (f32[12]{0:T(128)S(1)}, f32[1024]{0:T(1024)}) all-reduce(f32[12]{0:T(128)S(1)} %select_reduce_fusion, f32[1024]{0:T(1024)S(1)} %get-tuple-element.307), channel_id=1, replica_groups=mesh['dp'=8,'blk'=4] {'dp','blk'}, use_global_device_ids=true, to_apply=%region_30.31 | all-reduce | flops 1036 | bytes 8288 | tf_op jit(solution)/shard_map/psum | solution.py:269
  1619.5 6.2 fusion.49
  (208 shorter events, 36.0 us)
Async XLA Ops:
  7.2 11.5 copy-start.45
  7.2 11.9 copy-start.4
  7.2 290.0 %all-gather.6.cloned.1.call-start = ((), (), s32[]{:S(2)}) async-start(), calls=%async_computation.3 | async-start | bytes 51955200 | tf_op jit(solution)/shard_map/all_gather | solution.py:80
  18.5 557.1 %all-gather.4.cloned.1.call-start = ((), (), s32[]{:S(2)}) async-start(), calls=%async_computation.1 | async-start | bytes 5242880 | tf_op jit(solution)/shard_map/all_gather | solution.py:135
  19.2 504.3 %copy-start.33 = (f32[256]{0:T(256)}, f32[256]{0:T(256)S(1)}, u32[]{:S(2)}) copy-start(f32[256]{0:T(256)S(1)} %broadcast_multiply_fusion.1) | copy-start | bytes 3076
  19.5 426.9 %copy-start.39 = (f32[256]{0:T(256)}, f32[256]{0:T(256)S(1)}, u32[]{:S(2)}) copy-start(f32[256]{0:T(256)S(1)} %fusion.64) | copy-start | bytes 3076
  19.5 504.0 %copy-start.35 = (f32[256]{0:T(256)}, f32[256]{0:T(256)S(1)}, u32[]{:S(2)}) copy-start(f32[256]{0:T(256)S(1)} %fusion.90) | copy-start | bytes 3076
  506.6 16.9 %copy-start.29 = (f32[1024]{0:T(1024)}, f32[1024]{0:T(1024)S(1)}, u32[]{:S(2)}) copy-start(f32[1024]{0:T(1024)S(1)} %get-tuple-element.304) | copy-start | bytes 12292
  506.6 16.9 %copy-start.31 = (f32[1024]{0:T(1024)}, f32[1024]{0:T(1024)S(1)}, u32[]{:S(2)}) copy-start(f32[1024]{0:T(1024)S(1)} %get-tuple-element.303) | copy-start | bytes 12292
  528.2 1.1 copy-start.28
  530.6 241.7 %reduce-scatter.2.cloned.1.call-start = ((), (), s32[]{:S(2)}) async-start(), calls=%async_computation.2 | async-start | bytes 5242880 | tf_op jit(solution)/shard_map/reduce_scatter | solution.py:219
  542.7 3.3 slice-start
  604.9 5.8 copy-start
  620.5 5.8 copy-start
  632.0 2.7 copy-start.12
  632.0 19.7 %slice-start.9 = ((s8[8388608]{0:T(1024)(128)(4,1)}), s8[4194304]{0:T(1024)(128)(4,1)S(1)}, s32[]{:S(2)}) async-start(s8[8388608]{0:T(1024)(128)(4,1)} %bitcast.250), calls=%async_computation.14 | async-start | bytes 8388608
  634.7 31.4 %copy-start.6 = (f32[256,1024]{1,0:T(8,128)}, f32[256,1024]{1,0:T(8,128)S(1)}, u32[]{:S(2)}) copy-start(f32[256,1024]{1,0:T(8,128)S(1)} %get-tuple-element.310) | copy-start | bytes 3145732
  635.0 16.7 %slice-start.10 = ((s8[8388608]{0:T(1024)(128)(4,1)}), s8[4194304]{0:T(1024)(128)(4,1)S(1)}, s32[]{:S(2)}) async-start(s8[8388608]{0:T(1024)(128)(4,1)} %bitcast.250), calls=%async_computation.15 | async-start | bytes 8388608
  635.0 16.7 %copy-start.15 = (bf16[1,256,1024]{2,1,0:T(8,128)(2,1)S(1)}, bf16[1,256,1024]{2,1,0:T(8,128)(2,1)}, u32[]{:S(2)}) copy-start(bf16[1,256,1024]{2,1,0:T(8,128)(2,1)} %param.12) | copy-start | bytes 1572868
  658.7 7.4 copy-start.22
  666.0 3.0 copy-start.11
  666.1 4.0 copy-start.18
  674.3 6.4 copy-start.2
  684.6 5.8 copy-start.1
  690.4 2.2 copy-start.16
  690.4 4.4 copy-start.25
  692.8 2.0 copy-start.17
  698.7 6.4 copy-start.2
  709.3 5.8 copy-start.1
  715.1 2.2 copy-start.16
  715.1 4.4 copy-start.25
  717.6 2.0 copy-start.17
  729.3 1.2 copy-start.3
  729.3 1.4 copy-start.13
  729.3 1.5 copy-start.27
  729.3 827.9 %all-reduce.4.cloned.1.call-start = ((), (), s32[]{:S(2)}) async-start(), calls=%async_computation.4 | async-start | bytes 100761600
  731.5 3.0 copy-start.7
  731.5 3.0 copy-start.23
  737.1 7.0 copy-start.20
  746.4 25.8 %copy-start.5 = (bf16[1,256,1024]{2,1,0:T(8,128)(2,1)S(1)}, bf16[1,256,1024]{2,1,0:T(8,128)(2,1)}, u32[]{:S(2)}) copy-start(bf16[1,256,1024]{2,1,0:T(8,128)(2,1)} %param.11) | copy-start | bytes 1572868
  746.5 25.8 %copy-start.30 = (f32[1024]{0:T(1024)S(1)}, f32[1024]{0:T(1024)}, u32[]{:S(2)}) copy-start(f32[1024]{0:T(1024)} %copy-done.29) | copy-start | bytes 12292
  746.5 25.7 %copy-start.34 = (f32[256]{0:T(256)S(1)}, f32[256]{0:T(256)}, u32[]{:S(2)}) copy-start(f32[256]{0:T(256)} %copy-done.33) | copy-start | bytes 3076
  772.2 5.2 copy-start.40
  772.2 5.2 copy-start.36
  772.2 5.8 copy-start.10
  777.4 2.6 copy-start.19
  777.4 2.6 copy-start.32
  799.3 12.9 copy-start.8
  799.3 17.7 %slice-start.5 = ((s8[16777216]{0:T(1024)(128)(4,1)}), s8[4194304]{0:T(1024)(128)(4,1)S(1)}, s32[]{:S(2)}) async-start(s8[16777216]{0:T(1024)(128)(4,1)} %bitcast.243), calls=%async_computation.10 | async-start | bytes 8388608
  799.3 17.7 %slice-start.6 = ((s8[16777216]{0:T(1024)(128)(4,1)}), s8[4194304]{0:T(1024)(128)(4,1)S(1)}, s32[]{:S(2)}) async-start(s8[16777216]{0:T(1024)(128)(4,1)} %bitcast.243), calls=%async_computation.11 | async-start | bytes 8388608
  799.3 17.7 %slice-start.7 = ((s8[16777216]{0:T(1024)(128)(4,1)}), s8[4194304]{0:T(1024)(128)(4,1)S(1)}, s32[]{:S(2)}) async-start(s8[16777216]{0:T(1024)(128)(4,1)} %bitcast.243), calls=%async_computation.12 | async-start | bytes 8388608
  810.4 6.6 slice-start.8
  812.1 3.1 copy-start.37
  812.1 3.7 copy-start.43
  812.1 4.3 copy-start.42
  817.0 9.1 slice-start.1
  817.0 8.5 copy-start.38
  817.0 9.0 slice-start.2
  817.0 10.3 slice-start.3
  817.1 11.5 slice-start.4
  860.2 711.3 %copy-start.41 = (f32[1024]{0:T(1024)S(1)}, f32[1024]{0:T(1024)}, u32[]{:S(2)}) copy-start(f32[1024]{0:T(1024)} %get-tuple-element.297) | copy-start | bytes 12292
  1557.2 2.0 copy-start.14
  1557.2 14.3 copy-start.21
  1618.2 7.6 copy-start.46
  (5 other events, 4.0 us)
Sparse Core Ops, SparseCore 0:
  18.6 278.4 all-gather.5
  530.7 32.6 all-gather.3
  729.4 42.7 reduce-scatter.1
  835.3 721.8 all-reduce.3
where the time goes:
time: 1640 us; the launch traced here: 1630 us
  waiting for transfers between devices  991 us (60%)
  local copies, waits for them, and re-layouts  252 us (15%)
  other arithmetic  216 us (13%)
  matrix products  117 us (7%)
  blocking collectives  40 us (2%)
    unnamed x5, waiting for transfers between devices  696 us
    all_gather x1, waiting for transfers between devices, shards(): lax.all_gather(params.astype(jnp.bfloat16), ('dp', 'blk'), axis=0, tiled=...  278 us
    unnamed x120, local copies, waits for them, and re-layouts  153 us
    all_gather x1, other arithmetic, shards(): lax.all_gather(params.astype(jnp.bfloat16), ('dp', 'blk'), axis=0, tiled=...  149 us
    psum x1, blocking collectives, shards(): norms, bias_total = lax.psum((partials, grad_bias_down), ('dp', 'blk'))  40 us
    slice x6, local copies, waits for them, and re-layouts, unpack(): flat_params[marks[member]:marks[member + 1]]  34.1 us
  transfers between devices with their start and end apart: 4, of which 3 were waited for; matrix products, arithmetic and copies ran while one was open for 6% of the time, Pallas kernels for 0%

commit v1 on v0

--- a/solution.py
+++ b/solution.py
@@ -4,6 +4,8 @@
 import jax
 import jax.numpy as jnp
 from jax import lax
+from jax.experimental import pallas as pl
+from jax.experimental.pallas import tpu as pltpu
 from jax.sharding import PartitionSpec as P
 
 D = 1024
@@ -286,21 +288,1072 @@
     )
 
 
+MESH = pl.DeviceIdType.MESH
+LANE = 128
+
+
+def pick(cond, yes, no):
+    return jnp.where(cond, jnp.int32(yes), jnp.int32(no))
+
+
+def rdma(src, dst, ssem, rsem, dev):
+    return pltpu.make_async_remote_copy(src_ref=src, dst_ref=dst, send_sem=ssem, recv_sem=rsem, device_id=dev, device_id_type=MESH)
+
+
+def rows(ref, start, size, step=128):
+    return ref.at[pl.ds(pl.multiple_of(start, step), size)]
+
+
+def gate(peers):
+    sem = pltpu.get_barrier_semaphore()
+    for peer in peers:
+        pl.semaphore_signal(sem, inc=1, device_id=peer, device_id_type=MESH)
+    pl.semaphore_wait(sem, len(peers))
+
+
+class Place:
+    def __init__(self):
+        self.dp = lax.axis_index("dp")
+        self.blk = lax.axis_index("blk")
+        self.d = self.dp * 4 + self.blk
+        self.z = self.dp // 2
+        self.x = self.dp % 2
+        self.y = self.blk // 2
+        self.c = self.blk % 2
+        self.xpeer = (self.z * 2 + 1 - self.x, self.blk)
+        self.zs = [lax.rem(self.z + k, 4) for k in (1, 3, 2)]
+        self.zpeers = [(zz * 2 + self.x, self.blk) for zz in self.zs]
+        self.quad = [(self.dp, lax.rem(self.blk + k, 4)) for k in (1, 2, 3)]
+        up = lax.rem(self.d + 1, 32)
+        down = lax.rem(self.d + 31, 32)
+        self.next = (up // 4, up % 4)
+        self.prev = (down // 4, down % 4)
+        d = self.d
+        self.is_qkv = d < 8
+        self.is_out = (d == 8) | (d == 9)
+        self.is_mix_out = d == 10
+        self.is_up = (d >= 11) & (d < 21)
+        self.is_mix_down = d == 21
+        self.is_down = d >= 22
+        self.is_seg = self.is_out | self.is_down
+        self.is_mix = self.is_mix_out | self.is_mix_down
+        self.base = pick(d < 8, 16, pick(d < 11, 32, pick(d < 21, 56, 88))) - 3 * d
+        self.seg0 = pick(d < 11, 3 * (d - 8), jnp.maximum(3 * (d - 21) - 1, 0))
+        self.mix_up = pick(self.is_mix_out, 2074, -7)
+        self.mix_seg = pick(self.is_mix_out, 2, 1049)
+
+    def seg_home(self, n):
+        seg = self.seg0 + n // 4
+        panel = n % 4
+        out_row = 3072 + 256 * panel + 128 * (seg % 2)
+        down_row = 8192 + 1024 * panel + 128 * (seg // 4)
+        low = self.d < 11
+        return pick(low, seg // 2, seg % 4), pick(low, out_row, down_row)
+
+    def block_home(self, n):
+        part, row = self.seg_home(n)
+        return pick(self.is_qkv, n // 3, part), pick(self.is_qkv, (n % 3) * 1024 + 128 * self.d, row)
+
+    def up_home(self, n):
+        start = pick(self.is_up, 32 + 96 * (self.d - 11), pick(self.is_mix_out, 0, 992))
+        return n // 4, 4096 + 1024 * (n % 4) + start
+
+
+def chunk_row(q, k):
+    first = (k // 4) * 1024 + 512 * q + 128 * (k % 4)
+    turn = 3 * (q - 2) + k // 4
+    panel = k % 4
+    other = pick(
+        turn < 2,
+        3072 + 256 * panel + 128 * turn,
+        pick(turn < 10, 4096 + 1024 * panel + 128 * (turn - 2), 8192 + 1024 * panel + 128 * (turn - 10)),
+    )
+    return pick(q < 2, first, other)
+
+
+def loop(count, body):
+    def step(i, carry):
+        body(i)
+        return carry
+
+    lax.fori_loop(0, count, step, 0)
+
+
+def unit_span(start, stride):
+    return pl.ds(start, 16, stride=stride)
+
+
+def for_tiles(me, visit):
+    e0 = 24 + me.base
+
+    @pl.when(me.is_qkv)
+    def _():
+        def body(rb):
+            for ct in range(24):
+                n = ((ct % 8) // 2) * 3 + ct // 8
+                visit(e0 + 384 * rb + ct, 24, n * 128 + 16 * rb, 128 * (ct % 2))
+
+        loop(8, body)
+
+    @pl.when(me.is_up)
+    def _():
+        def body(rb):
+            for ct in range(32):
+                n = (ct % 4) * 4 + ct // 8
+                visit(e0 + 512 * rb + ct, 32, n * 96 + 16 * rb, 128 * ((ct // 4) % 2))
+
+        loop(6, body)
+
+    def segs(count, first):
+        def body(i):
+            for ct in range(8):
+                visit(first + 128 * i + ct, 8, ((i // 8) * 4 + ct // 2) * 128 + 16 * (i % 8), 128 * (ct % 2))
+
+        loop(count, body)
+
+    @pl.when(me.is_seg)
+    def _():
+        segs(24, e0)
+
+    @pl.when(me.is_mix)
+    def _():
+        segs(16, 24 + me.mix_seg)
+
+        def body(rb):
+            for ct in range(32):
+                n = (ct % 4) * 4 + ct // 8
+                visit(24 + me.mix_up + 512 * rb + ct, 32, 1024 + n * 32 + 16 * rb, 128 * ((ct // 4) % 2))
+
+        loop(2, body)
+
+
+def for_pieces(me, visit):
+    @pl.when(me.is_qkv | me.is_seg)
+    def _():
+        def body(n):
+            part, row = me.block_home(n)
+            visit(n, n * 128, 128, part, row, 128)
+
+        loop(12, body)
+
+    @pl.when(me.is_up)
+    def _():
+        def body(n):
+            part, row = me.up_home(n)
+            visit(n, n * 96, 96, part, row, 32)
+
+        loop(16, body)
+
+    @pl.when(me.is_mix)
+    def _():
+        def body(n):
+            part, row = me.seg_home(n)
+            visit(n, n * 128, 128, part, row, 128)
+
+        loop(8, body)
+
+        def body_up(n):
+            part, row = me.up_home(n)
+            visit(8 + n, 1024 + n * 32, 32, part, row, 32)
+
+        loop(16, body_up)
+
+
+def vec_spots(me, visit):
+    for cond, row, unit, count in (
+        (me.d == 0, 0, 0, 16),
+        (me.d == 7, 0, 3067, 8),
+        (me.d == 8, 0, 0, 8),
+        (me.d == 10, 8, 2050, 24),
+        (me.d == 21, 0, 1017, 32),
+        (me.d == 31, 0, 3067, 8),
+    ):
+
+        @pl.when(cond)
+        def _(row=row, unit=unit, count=count):
+            visit(row, 24 + unit, count)
+
+
+def send_rows(me, src, dst, ssem, rsem):
+    mine = pl.ds(pl.multiple_of(me.blk * 256, 256), 256)
+    return [rdma(src, dst.at[mine], ssem, rsem, peer) for peer in me.quad]
+
+
+def gather(me, r):
+    gate(me.quad + me.zpeers + [me.xpeer, me.next, me.prev])
+    r.tail[...] = r.par[3051:3075, :]
+    up = rdma(r.tail, r.hp, r.hsem.at[0], r.hsem.at[1], me.next)
+    down = rdma(r.par.at[0:24], r.hn, r.hsem.at[2], r.hsem.at[3], me.prev)
+    up.start()
+    down.start()
+    sends = send_rows(me, r.pat, r.PA, r.asem.at[0], r.asem.at[1]) + send_rows(me, r.cot, r.CA, r.asem.at[2], r.asem.at[3])
+    mine = pl.ds(pl.multiple_of(me.blk * 256, 256), 256)
+    r.PA[mine, :] = r.pat[...]
+    r.CA[mine, :] = r.cot[...]
+
+    def put(i):
+        r.E[pl.ds(pl.multiple_of(24 + 64 * i, 8), 64), :] = r.par[pl.ds(pl.multiple_of(64 * i, 8), 64), :]
+
+    loop(48, put)
+    r.E[3096:3099, :] = r.par[3072:3075, :]
+    up.wait()
+    down.wait()
+    r.E[0:24, :] = r.hp[...]
+    r.E[3099:3123, :] = r.hn[...]
+
+    def tile(unit, stride, row, lane):
+        r.S[pl.ds(pl.multiple_of(row, 16), 16), lane : lane + 128] = r.E[unit_span(unit, stride), :].astype(jnp.bfloat16)
+
+    for_tiles(me, tile)
+    r.VS[...] = jnp.zeros_like(r.VS)
+
+    def vec(row, unit, count):
+        r.VS[row : row + count, :] = r.E[unit : unit + count, :].astype(jnp.bfloat16).astype(jnp.float32)
+
+    vec_spots(me, vec)
+
+    def piece(go):
+        def visit(i, srow, size, part, frow, step):
+            src = rows(r.S, srow, size, 32)
+            dst = rows(r.F, frow, size, step)
+
+            @pl.when(part != me.blk)
+            def _():
+                cp = rdma(src, dst, r.qsem.at[i], r.csem, (me.dp, part))
+                cp.start() if go else cp.wait_send()
+
+            if go:
+
+                @pl.when(part == me.blk)
+                def _():
+                    pltpu.make_async_copy(src, dst, r.csem).start()
+
+        return visit
+
+    vq = [rdma(r.VS, r.VQ.at[me.blk], r.vsem.at[0], r.vsem.at[1], peer) for peer in me.quad]
+    for v in vq:
+        v.start()
+    for_pieces(me, piece(True))
+    r.VQ[me.blk] = r.VS[...]
+    pltpu.make_async_copy(r.VQ.at[0:3], r.VQ.at[0:3], r.vsem.at[0]).wait()
+    pltpu.make_async_copy(r.VQ.at[0:3], r.VQ.at[0:3], r.vsem.at[1]).wait()
+    r.XV[me.dp] = r.VQ[0] + r.VQ[1] + r.VQ[2] + r.VQ[3]
+    pltpu.make_async_copy(r.F.at[0:1536], r.F.at[0:1536], r.csem).wait()
+
+    def block(q, k):
+        return rows(r.F, chunk_row(q, k), 128)
+
+    def xsend(q, zsrc, g):
+        for i in range(4):
+            ref = block(q, g * 4 + i)
+            rdma(ref, ref, r.xs, r.xr.at[zsrc * 3 + g], me.xpeer).start()
+
+    def vsend(q, zsrc):
+        rdma(r.XV.at[q], r.XV.at[q], r.vxs, r.vxr.at[zsrc], me.xpeer).start()
+
+    for g in range(3):
+        for i in range(4):
+            ref = block(me.dp, g * 4 + i)
+            for peer in me.zpeers:
+                rdma(ref, ref, r.zs, r.zr.at[me.z * 3 + g], peer).start()
+        xsend(me.dp, me.z, g)
+    for peer in me.zpeers:
+        rdma(r.XV.at[me.dp], r.XV.at[me.dp], r.vzs, r.vzr.at[me.z], peer).start()
+    vsend(me.dp, me.z)
+
+    for s in sends:
+        s.start()
+
+    def arrived(ref, sem):
+        pltpu.make_async_copy(ref, ref, sem).wait()
+
+    four = r.F.at[0:512]
+    for g in range(3):
+        for zz in me.zs:
+            arrived(four, r.zr.at[zz * 3 + g])
+            xsend(zz * 2 + me.x, zz, g)
+    for zz in me.zs:
+        arrived(r.XV.at[0], r.vzr.at[zz])
+        vsend(zz * 2 + me.x, zz)
+    for zz in [me.z] + me.zs:
+        arrived(r.XV.at[0], r.vxr.at[zz])
+        for g in range(3):
+            arrived(four, r.xr.at[zz * 3 + g])
+    arrived(r.F.at[0:4608], r.zs)
+    arrived(r.F.at[0:6144], r.xs)
+    arrived(r.XV.at[0:3], r.vzs)
+    arrived(r.XV.at[0:4], r.vxs)
+    for_pieces(me, piece(False))
+    for i in range(4):
+        arrived(r.PA.at[0:768], r.asem.at[i])
+
+
+GATHER_SCRATCH = dict(
+    E=pltpu.VMEM((3128, 128), jnp.float32),
+    tail=pltpu.VMEM((24, 128), jnp.float32),
+    hp=pltpu.VMEM((24, 128), jnp.float32),
+    hn=pltpu.VMEM((24, 128), jnp.float32),
+    S=pltpu.VMEM((1536, 256), jnp.bfloat16),
+    VS=pltpu.VMEM((32, 128), jnp.float32),
+    VQ=pltpu.VMEM((4, 32, 128), jnp.float32),
+    hsem=pltpu.SemaphoreType.DMA((4,)),
+    asem=pltpu.SemaphoreType.DMA((4,)),
+    qsem=pltpu.SemaphoreType.DMA((24,)),
+    csem=pltpu.SemaphoreType.DMA,
+    vsem=pltpu.SemaphoreType.DMA((2,)),
+    xs=pltpu.SemaphoreType.DMA,
+    xr=pltpu.SemaphoreType.DMA((12,)),
+    zs=pltpu.SemaphoreType.DMA,
+    zr=pltpu.SemaphoreType.DMA((12,)),
+    vxs=pltpu.SemaphoreType.DMA,
+    vxr=pltpu.SemaphoreType.DMA((4,)),
+    vzs=pltpu.SemaphoreType.DMA,
+    vzr=pltpu.SemaphoreType.DMA((4,)),
+)
+
+
+class Refs:
+    pass
+
+
+def call(phase, ins, outs, scratch, cid, args):
+    names = list(ins) + list(outs) + list(scratch)
+
+    def kernel(*refs):
+        r = Refs()
+        for name, ref in zip(names, refs):
+            setattr(r, name, ref)
+        phase(Place(), r)
+
+    whole = pl.BlockSpec(memory_space=pltpu.VMEM)
+    return pl.pallas_call(
+        kernel,
+        out_shape=[jax.ShapeDtypeStruct(*o) for o in outs.values()],
+        in_specs=[whole] * len(ins),
+        out_specs=[whole] * len(outs),
+        scratch_shapes=list(scratch.values()),
+        compiler_params=pltpu.CompilerParams(collective_id=cid, has_side_effects=True, vmem_limit_bytes=62 * 2**20),
+    )(*args)
+
+
+def k1(par, pat, cot):
+    return call(
+        gather,
+        ("par", "pat", "cot"),
+        dict(
+            F=((12288, 256), jnp.bfloat16),
+            XV=((8, 32, 128), jnp.float32),
+            PA=((1024, 1024), jnp.bfloat16),
+            CA=((1024, 1024), jnp.bfloat16),
+        ),
+        GATHER_SCRATCH,
+        0,
+        (par, pat, cot),
+    )
+
+
+BF, F32 = jnp.bfloat16, jnp.float32
+EPS = 1e-06
+OUT0, UP0, DOWN0 = 3072, 4096, 8192
+
+
+def dot(a, b):
+    return lax.dot_general(a, b, (((1,), (0,)), ((), ())), preferred_element_type=F32)
+
+
+def dot_nt(a, b):
+    return lax.dot_general(a, b, (((1,), (1,)), ((), ())), preferred_element_type=F32)
+
+
+def dot_tn(a, b):
+    return lax.dot_general(a, b, (((0,), (0,)), ((), ())), preferred_element_type=F32)
+
+
+def block_of(i):
+    return pl.ds(pl.multiple_of(i * 256, 256), 256)
+
+
+def wide(r, q, first, count=8):
+    return jnp.concatenate([r.XV[q, first + i : first + i + 1, :] for i in range(count)], axis=1)
+
+
+def narrow(r, q, first):
+    return jnp.concatenate([r.XV[q, pl.ds(first + i, 1), :] for i in range(2)], axis=1)
+
+
+def put_vec(r, q, first, row, add=False):
+    for i in range(row.shape[1] // 128):
+        part = row[:, i * 128 : i * 128 + 128]
+        if add:
+            part = part + r.VG[q, first + i : first + i + 1, :]
+        r.VG[q, first + i : first + i + 1, :] = part
+
+
+def normalize(x):
+    mean = jnp.mean(x, axis=-1, keepdims=True)
+    cen = x - mean
+    var = jnp.mean(cen * cen, axis=-1, keepdims=True)
+    scale = lax.rsqrt(var + EPS)
+    return cen * scale, scale
+
+
+def norm_back(dy, xhat, scale, gain):
+    t = dy * gain
+    return scale * (t - jnp.mean(t, axis=-1, keepdims=True) - xhat * jnp.mean(t * xhat, axis=-1, keepdims=True))
+
+
+def quad_sum(me, r, make, sems, finish, slot=2):
+    y, c = me.y, me.c
+    sib, yp = (me.dp, y * 2 + 1 - c), (me.dp, (1 - y) * 2 + c)
+    far_sib, far, near_sib, own = (1 - y) * 2 + 1 - c, (1 - y) * 2 + c, y * 2 + 1 - c, me.blk
+    ssem, rsem = sems
+    make(far_sib)
+    a = rdma(r.PB.at[block_of(far_sib)], r.RB.at[0], ssem.at[0], rsem.at[0], sib)
+    a.start()
+    make(far)
+    a.wait_recv()
+    for i in range(4):
+        at = pl.ds(pl.multiple_of(far * 256 + 64 * i, 64), 64)
+        lo = slice(64 * i, 64 * i + 64)
+        r.RB[3, lo, :] = (r.PB[at, :].astype(F32) + r.RB[0, lo, :].astype(F32)).astype(BF)
+    b = rdma(r.RB.at[3], r.RB.at[slot], ssem.at[1], rsem.at[1], yp)
+    b.start()
+    make(near_sib)
+    d = rdma(r.PB.at[block_of(near_sib)], r.RB.at[1], ssem.at[2], rsem.at[2], sib)
+    d.start()
+    make(own)
+    d.wait_recv()
+    b.wait_recv()
+    for i in range(4):
+        at = pl.ds(pl.multiple_of(own * 256 + 64 * i, 64), 64)
+        lo = slice(64 * i, 64 * i + 64)
+        finish(lo, r.PB[at, :].astype(F32) + r.RB[1, lo, :].astype(F32) + r.RB[slot, lo, :].astype(F32))
+    a.wait_send()
+    b.wait_send()
+    d.wait_send()
+
+
+def quad_share(me, r, buf, sems):
+    y, c = me.y, me.c
+    sib, yp = (me.dp, y * 2 + 1 - c), (me.dp, (1 - y) * 2 + c)
+    ssem, rsem = sems
+
+    def part(dev, i):
+        return buf.at[pl.ds(pl.multiple_of(dev * 256 + 64 * i, 64), 64)]
+
+    far = (1 - y) * 2 + c
+    over = [rdma(part(me.blk, i), part(me.blk, i), ssem.at[i], rsem.at[i], yp) for i in range(4)]
+    near = rdma(buf.at[block_of(me.blk)], buf.at[block_of(me.blk)], ssem.at[8], rsem.at[8], sib)
+    pass_on = [rdma(part(far, i), part(far, i), ssem.at[4 + i], rsem.at[4 + i], sib) for i in range(4)]
+    for o in over:
+        o.start()
+    near.start()
+    for i in range(4):
+        over[i].wait_recv()
+        pass_on[i].start()
+    near.wait()
+    for i in range(4):
+        over[i].wait_send()
+        pass_on[i].wait()
+
+
+def labels_at(r, at):
+    total = jnp.zeros_like(at)
+    bound = 0
+    for k in range(9):
+        bound = bound + r.lens[k]
+        total = total + (at >= bound).astype(jnp.int32)
+    return total
+
+
+def lane_mask(h):
+    lane = lax.broadcasted_iota(jnp.int32, (1, 128), 1)
+    return ((lane // 64) == h).astype(BF)
+
+
+def forward_a(me, r):
+    gain, shift = wide(r, 0, 0), wide(r, 0, 8)
+
+    def ln(i):
+        at = pl.ds(pl.multiple_of(i * 64, 64), 64)
+        xhat, _ = normalize(r.PA[at, :].astype(F32))
+        r.NO[at, :] = (xhat * gain + shift).astype(BF)
+
+    loop(16, ln)
+    bias = [narrow(r, 1, 2 * me.blk), None, narrow(r, 2, 2 * me.blk)]
+
+    def proj(i):
+        at = block_of(i)
+        for j in range(3):
+            out = dot(r.NO[at, :], r.F[j * 1024 : j * 1024 + 1024, :])
+            if bias[j] is not None:
+                out = out + bias[j]
+            r.QKV[j, at, :] = out.astype(BF)
+
+    loop(4, proj)
+    key_labels = labels_at(r, lax.broadcasted_iota(jnp.int32, (1, 1024), 1))
+
+    def attend(i):
+        at = block_of(i)
+        row_labels = labels_at(r, lax.broadcasted_iota(jnp.int32, (256, 1), 0) + i * 256)
+        allowed = row_labels == key_labels
+        for t in range(2):
+            lanes = slice(128 * t, 128 * t + 128)
+            q = r.QKV[0, at, lanes]
+            k = r.QKV[1, :, lanes]
+            v = r.QKV[2, :, lanes]
+            out = jnp.zeros((256, 128), F32)
+            for h in range(2):
+                m = lane_mask(h)
+                s = jnp.where(allowed, dot_nt(q * m, k) * 0.125, -1e30)
+                w = jnp.exp(s - jnp.max(s, axis=-1, keepdims=True))
+                p = (w * (1.0 / jnp.sum(w, axis=-1, keepdims=True))).astype(BF)
+                r.P[2 * t + h, at, :] = p
+                out = out + dot(p, v * m)
+            r.AT[at, lanes] = out.astype(BF)
+
+    loop(4, attend)
+
+
+def forward_b(me, r):
+    def term(i):
+        at = block_of(i)
+        for p in range(4):
+            r.PB[at, 256 * p : 256 * p + 256] = dot(r.AT[at, :], r.F[OUT0 + 256 * p : OUT0 + 256 * p + 256, :]).astype(BF)
+
+    bias_out = wide(r, 2, 8)
+    gain, shift = wide(r, 2, 16), wide(r, 2, 24)
+
+    def finish(lo, total):
+        x = r.pat[lo, :].astype(F32) + (total + bias_out)
+        r.MID[lo, :] = x
+        xhat, _ = normalize(x)
+        r.NT[pl.ds(pl.multiple_of(me.blk * 256 + lo.start, 64), 64), :] = (xhat * gain + shift).astype(BF)
+
+    quad_sum(me, r, term, (r.s1s, r.s1r), finish)
+    quad_share(me, r, r.NT, (r.g1s, r.g1r))
+
+
+def forward_c(me, r):
+    biases = [jnp.concatenate([r.XV[5, pl.ds(4 * (2 * p + i) + me.blk, 1), :] for i in range(2)], axis=1) for p in range(4)]
+
+    def up(i):
+        at = pl.ds(pl.multiple_of(i * 128, 128), 128)
+        for p in range(4):
+            h = dot(r.NT[at, :], r.F[UP0 + 1024 * p : UP0 + 1024 * p + 1024, :]) + biases[p]
+            phi = 0.5 + 0.5 * lax.erf(h * 0.7071067811865476)
+            lanes = slice(256 * p, 256 * p + 256)
+            r.AC[at, lanes] = (h * phi).astype(BF)
+            r.GP[at, lanes] = (phi + h * (jnp.exp(-0.5 * h * h) * 0.3989422804014327)).astype(BF)
+
+    loop(8, up)
+
+
+def forward_d(me, r):
+    def term(i):
+        at = block_of(i)
+        for p in range(4):
+            r.PB[at, 256 * p : 256 * p + 256] = dot(r.AC[at, :], r.F[DOWN0 + 1024 * p : DOWN0 + 1024 * p + 1024, :]).astype(BF)
+
+    bias_down = wide(r, 7, 0)
+
+    def finish(lo, total):
+        r.act[lo, :] = (r.MID[lo, :] + (total + bias_down)).astype(BF)
+
+    quad_sum(me, r, term, (r.s2s, r.s2r), finish, 4)
+
+
+def backward_a(me, r):
+    r.VG[...] = jnp.zeros_like(r.VG)
+
+    def hidden(i):
+        at = block_of(i)
+        for p in range(4):
+            lanes = slice(256 * p, 256 * p + 256)
+            acc = jnp.zeros((256, 256), F32)
+            for k in range(4):
+                acc = acc + dot_nt(r.CA[at, 256 * k : 256 * k + 256], r.F[DOWN0 + 1024 * k + 256 * p : DOWN0 + 1024 * k + 256 * p + 256, :])
+            r.GH[at, lanes] = (acc * r.GP[at, lanes].astype(F32)).astype(BF)
+
+    loop(4, hidden)
+    for p in range(4):
+        sums = jnp.sum(r.GH[:, 256 * p : 256 * p + 256].astype(F32), axis=0, keepdims=True)
+        for i in range(2):
+            r.VG[5, pl.ds(4 * (2 * p + i) + me.blk, 1), :] = sums[:, 128 * i : 128 * i + 128]
+    put_vec(r, 7, 0, jnp.sum(r.cot[...].astype(F32), axis=0, keepdims=True))
+
+
+def weight_grad(r, left, right, base, height):
+    def body(i):
+        cols = pl.ds(pl.multiple_of(i * 256, 256), 256)
+        lt = left[:, cols].T
+        for p in range(right.shape[1] // 256):
+            out = dot(lt, right[:, 256 * p : 256 * p + 256])
+            r.G[pl.ds(pl.multiple_of(base + p * height + i * 256, 256), 256), :] = out.astype(BF)
+
+    loop(height // 256, body)
+
+
+def backward_b(me, r):
+    weight_grad(r, r.AC, r.CA, DOWN0, 1024)
+    weight_grad(r, r.NT, r.GH, UP0, 1024)
+
+
+def backward_c(me, r):
+    def term(i):
+        at = block_of(i)
+        for n in range(4):
+            acc = jnp.zeros((256, 256), F32)
+            for p in range(4):
+                acc = acc + dot_nt(r.GH[at, 256 * p : 256 * p + 256], r.F[UP0 + 1024 * p + 256 * n : UP0 + 1024 * p + 256 * n + 256, :])
+            r.PB[at, 256 * n : 256 * n + 256] = acc.astype(BF)
+
+    gain = wide(r, 2, 16)
+    sums = [jnp.zeros((1, 1024), F32)] * 3
+
+    def finish(lo, dy):
+        xhat, scale = normalize(r.MID[lo, :])
+        gm = r.cot[lo, :].astype(F32) + norm_back(dy, xhat, scale, gain)
+        r.MID[lo, :] = gm
+        low = gm.astype(BF)
+        r.GM[pl.ds(pl.multiple_of(me.blk * 256 + lo.start, 64), 64), :] = low
+        for n, term_of in enumerate((low.astype(F32), dy * xhat, dy)):
+            sums[n] = sums[n] + jnp.sum(term_of, axis=0, keepdims=True)
+
+    quad_sum(me, r, term, (r.s3s, r.s3r), finish)
+    quad_share(me, r, r.GM, (r.g2s, r.g2r))
+    for n in range(3):
+        put_vec(r, 2, 8 + 8 * n, sums[n])
+
+
+def backward_d(me, r):
+    weight_grad(r, r.AT, r.GM, OUT0, 256)
+
+    def attended(i):
+        at = block_of(i)
+        acc = jnp.zeros((256, 256), F32)
+        for p in range(4):
+            acc = acc + dot_nt(r.GM[at, 256 * p : 256 * p + 256], r.F[OUT0 + 256 * p : OUT0 + 256 * p + 256, :])
+        r.DA[at, :] = acc.astype(BF)
+
+    loop(4, attended)
+    r.KV[...] = jnp.zeros_like(r.KV)
+
+    def attend(i):
+        at = block_of(i)
+        for t in range(2):
+            lanes = slice(128 * t, 128 * t + 128)
+            q = r.QKV[0, at, lanes]
+            k = r.QKV[1, :, lanes]
+            v = r.QKV[2, :, lanes]
+            da = r.DA[at, lanes]
+            dq = jnp.zeros((256, 128), F32)
+            for h in range(2):
+                m = lane_mask(h)
+                p = r.P[2 * t + h, at, :]
+                pf = p.astype(F32)
+                dp = dot_nt(da * m, v)
+                delta = jnp.sum(pf * dp, axis=-1, keepdims=True)
+                ds = (pf * (dp - delta) * 0.125).astype(BF)
+                dq = dq + dot(ds, k * m)
+                r.KV[0, :, lanes] += dot_tn(ds, q * m)
+                r.KV[1, :, lanes] += dot_tn(p, da * m)
+            r.DQ[0, at, lanes] = dq.astype(BF)
+
+    loop(4, attend)
+    r.DQ[1] = r.KV[0].astype(BF)
+    r.DQ[2] = r.KV[1].astype(BF)
+    for j, q in ((0, 1), (2, 2)):
+        sums = jnp.sum(r.DQ[j].astype(F32), axis=0, keepdims=True)
+        for i in range(2):
+            r.VG[q, pl.ds(2 * me.blk + i, 1), :] = sums[:, 128 * i : 128 * i + 128]
+
+
+def backward_e(me, r):
+    def body(i):
+        cols = pl.ds(pl.multiple_of(i * 256, 256), 256)
+        lt = r.NO[:, cols].T
+        for j in range(3):
+            r.G[pl.ds(pl.multiple_of(j * 1024 + i * 256, 256), 256), :] = dot(lt, r.DQ[j]).astype(BF)
+
+    loop(4, body)
+
+
+def backward_f(me, r):
+    def term(i):
+        at = block_of(i)
+        for n in range(4):
+            acc = jnp.zeros((256, 256), F32)
+            for j in range(3):
+                acc = acc + dot_nt(r.DQ[j, at, :], r.F[1024 * j + 256 * n : 1024 * j + 256 * n + 256, :])
+            r.PB[at, 256 * n : 256 * n + 256] = acc.astype(BF)
+
+    gain = wide(r, 0, 0)
+    sums = [jnp.zeros((1, 1024), F32)] * 2
+
+    def finish(lo, dy):
+        xhat, scale = normalize(r.pat[lo, :].astype(F32))
+        r.ing[lo, :] = (r.MID[lo, :] + norm_back(dy, xhat, scale, gain)).astype(BF)
+        for n, term_of in enumerate((dy * xhat, dy)):
+            sums[n] = sums[n] + jnp.sum(term_of, axis=0, keepdims=True)
+
+    quad_sum(me, r, term, (r.s4s, r.s4r), finish, 4)
+    for n in range(2):
+        put_vec(r, 0, 8 * n, sums[n])
+
+
+def compute(me, r):
+    gate(me.quad)
+    for phase in (forward_a, forward_b, forward_c, forward_d, backward_a, backward_b, backward_c, backward_d, backward_e, backward_f):
+        phase(me, r)
+
+
+DMA = pltpu.SemaphoreType.DMA
+COMPUTE_SCRATCH = dict(
+    NO=pltpu.VMEM((1024, 1024), BF),
+    QKV=pltpu.VMEM((3, 1024, 256), BF),
+    P=pltpu.VMEM((4, 1024, 1024), BF),
+    AT=pltpu.VMEM((1024, 256), BF),
+    PB=pltpu.VMEM((1024, 1024), BF),
+    RB=pltpu.VMEM((5, 256, 1024), BF),
+    MID=pltpu.VMEM((256, 1024), F32),
+    NT=pltpu.VMEM((1024, 1024), BF),
+    AC=pltpu.VMEM((1024, 1024), BF),
+    GP=pltpu.VMEM((1024, 1024), BF),
+    GH=pltpu.VMEM((1024, 1024), BF),
+    GM=pltpu.VMEM((1024, 1024), BF),
+    DA=pltpu.VMEM((1024, 256), BF),
+    KV=pltpu.VMEM((2, 1024, 256), F32),
+    DQ=pltpu.VMEM((3, 1024, 256), BF),
+    s1s=DMA((3,)), s1r=DMA((3,)), s2s=DMA((3,)), s2r=DMA((3,)), s3s=DMA((3,)), s3r=DMA((3,)), s4s=DMA((3,)), s4r=DMA((3,)),
+    g1s=DMA((9,)), g1r=DMA((9,)), g2s=DMA((9,)), g2r=DMA((9,)),
+)
+
+
+def k2(lens, pat, cot, F, XV, PA, CA):
+    ins = ("lens", "pat", "cot", "F", "XV", "PA", "CA")
+    outs = dict(G=((12288, 256), BF), VG=((8, 32, 128), F32), act=((256, 1024), BF), ing=((256, 1024), BF))
+    names = list(ins) + list(outs) + list(COMPUTE_SCRATCH)
+
+    def kernel(*refs):
+        r = Refs()
+        for name, ref in zip(names, refs):
+            setattr(r, name, ref)
+        compute(Place(), r)
+
+    whole = pl.BlockSpec(memory_space=pltpu.VMEM)
+    return pl.pallas_call(
+        kernel,
+        out_shape=[jax.ShapeDtypeStruct(*o) for o in outs.values()],
+        in_specs=[pl.BlockSpec(memory_space=pltpu.SMEM)] + [whole] * 6,
+        out_specs=[whole] * len(outs),
+        scratch_shapes=list(COMPUTE_SCRATCH.values()),
+        compiler_params=pltpu.CompilerParams(collective_id=1, has_side_effects=True, vmem_limit_bytes=62 * 2**20),
+    )(lens, pat, cot, F, XV, PA, CA)
+
+
+def crow(q, k):
+    return pick(q < 2, 128 * k, 384 * (k % 4) + 128 * (k // 4))
+
+
+class Other(Place):
+    def __init__(self, me, i):
+        d = me.dp * 4 + i
+        self.d, self.blk, self.dp = d, i, me.dp
+        self.is_qkv = d < 8
+        self.is_out = (d == 8) | (d == 9)
+        self.is_mix_out = d == 10
+        self.is_up = (d >= 11) & (d < 21)
+        self.is_mix_down = d == 21
+        self.is_down = d >= 22
+        self.is_seg = self.is_out | self.is_down
+        self.is_mix = self.is_mix_out | self.is_mix_down
+        self.seg0 = pick(d < 11, 3 * (d - 8), jnp.maximum(3 * (d - 21) - 1, 0))
+
+    def seg_spot(self, n):
+        seg = self.seg0 + n // 4
+        low = self.d < 11
+        turn = pick(low, seg % 2, 10 + seg // 4 - 3 * (self.dp - 2))
+        return pick(low, seg // 2, seg % 4), 384 * (n % 4) + 128 * turn
+
+    def block_spot(self, n):
+        part, row = self.seg_spot(n)
+        return pick(self.is_qkv, n // 3, part), pick(self.is_qkv, (n % 3) * 512 + 128 * (self.d % 4), row)
+
+    def up_spot(self, n):
+        start = pick(self.is_up, 32 + 96 * (self.d - 11), pick(self.is_mix_out, 0, 992))
+        return n // 4, 384 * (n % 4) + 256 + start - 384 * (self.dp - 2)
+
+    def pieces(self, visit):
+        @pl.when(self.is_qkv | self.is_seg)
+        def _():
+            loop(12, lambda n: visit(n, n * 128, 128, *self.block_spot(n)))
+
+        @pl.when(self.is_up)
+        def _():
+            loop(16, lambda n: visit(n, n * 96, 96, *self.up_spot(n)))
+
+        @pl.when(self.is_mix)
+        def _():
+            loop(8, lambda n: visit(n, n * 128, 128, *self.seg_spot(n)))
+            loop(16, lambda n: visit(8 + n, 1024 + n * 32, 32, *self.up_spot(n)))
+
+
+def arrived(ref, sem):
+    pltpu.make_async_copy(ref, ref, sem).wait()
+
+
+def squares(x):
+    s = jnp.sum(x * x, axis=0, keepdims=True)
+    return s[:, :128] + s[:, 128:] if x.shape[1] == 256 else s
+
+
+def reduce_x(me, r, zz, groups=(0, 1, 2)):
+    q = zz * 2 + 1 - me.x
+    for g in groups:
+        for i in range(4):
+            k = g * 4 + i
+            rdma(rows(r.G, chunk_row(q, k), 128), rows(r.XR.at[zz], crow(q, k), 128), r.rxs, r.rxr.at[zz * 3 + g], me.xpeer).start()
+
+
+def reduce_z(me, r, zz, g):
+    q = zz * 2 + me.x
+    arrived(r.G.at[0:512], r.rxr.at[zz * 3 + g])
+    for i in range(4):
+        k = g * 4 + i
+        src, at = pl.ds(pl.multiple_of(chunk_row(q, k), 128), 128), pl.ds(pl.multiple_of(crow(q, k), 128), 128)
+        total = r.G[src, :].astype(F32) + r.XR[zz, at, :].astype(F32)
+        r.XR[zz, at, :] = total.astype(BF)
+
+        @pl.when(me.z != zz)
+        def _():
+            rdma(rows(r.XR.at[zz], crow(q, k), 128), rows(r.ZR.at[me.z], crow(q, k), 128), r.rzs.at[zz], r.rzr.at[me.z * 3 + g], (q, me.blk)).start()
+
+
+def reduce_phase(me, r):
+    for zz in (3, 2, 1, 0):
+        reduce_x(me, r, zz)
+    for zz in range(4):
+        rdma(r.VG.at[zz * 2 + 1 - me.x], r.VX.at[zz], r.wxs, r.wxr.at[zz], me.xpeer).start()
+    for zz in (3, 2, 1, 0):
+        for g in range(3):
+            reduce_z(me, r, zz, g)
+    reduce_vectors(me, r)
+    finish_chunk(me, r)
+
+
+def reduce_vectors(me, r):
+    for zz in range(4):
+        arrived(r.VX.at[0], r.wxr.at[zz])
+        r.VX[zz] = r.VX[zz] + r.VG[zz * 2 + me.x]
+
+        @pl.when(me.z != zz)
+        def _():
+            rdma(r.VX.at[zz], r.VZ.at[me.z], r.wzs.at[zz], r.wzr.at[me.z], (zz * 2 + me.x, me.blk)).start()
+
+    total = r.VX[me.z]
+    for zz in me.zs:
+        arrived(r.VZ.at[0], r.wzr.at[zz])
+        total = total + r.VZ[zz]
+    r.VT[me.blk] = total
+    outs = [rdma(r.VT.at[me.blk], r.VT.at[me.blk], r.wqs, r.wqr.at[me.blk], peer) for peer in me.quad]
+    for o in outs:
+        o.start()
+    for k in (1, 2, 3):
+        arrived(r.VT.at[0], r.wqr.at[lax.rem(me.blk + k, 4)])
+    r.VS[...] = r.VT[0] + r.VT[1] + r.VT[2] + r.VT[3]
+
+
+def finish_chunk(me, r):
+    r.NB[0] = jnp.zeros((24, 128), F32)
+    first_tensor = pick(me.dp < 2, 2, pick(me.dp == 2, 4, pick(me.dp < 6, 8, 10)))
+    for g in range(3):
+        for zz in me.zs:
+            arrived(r.G.at[0:512], r.rzr.at[zz * 3 + g])
+        part = jnp.zeros((1, 128), F32)
+        for i in range(4):
+            at = pl.ds(pl.multiple_of(crow(me.dp, g * 4 + i), 128), 128)
+            total = r.XR[me.z, at, :].astype(F32)
+            for zz in me.zs:
+                total = total + r.ZR[zz, at, :].astype(F32)
+            part = part + squares(total)
+            r.C[at, :] = total.astype(BF)
+        tensor = first_tensor
+        if g == 2:
+            tensor = pick(me.dp == 2, 8, tensor)
+        if g >= 1:
+            tensor = pick(me.dp == 5, 10, tensor)
+        r.NB[0, pl.ds(tensor, 1), :] += part
+    for i in range(4):
+        def visit(n, srow, size, part, row, i=i):
+            src, dst = rows(r.C, row, size, 32), rows(r.S, srow, size, 32)
+
+            @pl.when((part == me.blk) & (me.blk != i))
+            def _():
+                rdma(src, dst, r.qsem2.at[i * 24 + n], r.csem2, (me.dp, i)).start()
+
+            @pl.when((part == me.blk) & (me.blk == i))
+            def _():
+                pltpu.make_async_copy(src, dst, r.csem2).start()
+
+        Other(me, i).pieces(visit)
+    for q, tensors in ((0, (0, 1, None, None)), (1, (3, None, None, None)), (2, (3, 5, 6, 7)), (5, (9, 9, 9, 9)), (7, (11, None, None, None))):
+        @pl.when((me.dp == q) & (me.blk == 0))
+        def _(q=q, tensors=tensors):
+            for g, tensor in enumerate(tensors):
+                if tensor is not None:
+                    r.NB[0, tensor : tensor + 1, :] += squares(r.VS[8 * g : 8 * g + 8, :])
+            if q == 7:
+                r.NB[0, 16:24, :] = r.VS[0:8, :]
+
+
+def norm_exchange(me, r):
+    zx = [(me.z + 1 - 2 * (me.z % 2)), lax.rem(me.z + 2, 4)]
+    peers = [(me.dp, me.y * 2 + 1 - me.c), (me.dp, (1 - me.y) * 2 + me.c), me.xpeer] + [(z * 2 + me.x, me.blk) for z in zx]
+    for n, peer in enumerate(peers):
+        cp = rdma(r.NB.at[n], r.NR.at[n], r.nsem.at[n], r.nrsem.at[n], peer)
+        cp.start()
+        cp.wait()
+        r.NB[n + 1] = r.NB[n] + r.NR[n]
+
+
+def units_phase(me, r):
+    arrived(r.S, r.csem2)
+
+    def clear(i):
+        r.E[pl.ds(pl.multiple_of(i * 8, 8), 8), :] = jnp.zeros((8, 128), F32)
+
+    for i in (0, 1, 2, 3, 4, 5, 385, 386, 387, 388, 389, 390):
+        clear(i)
+
+    def tile(unit, stride, row, lane):
+        r.E[unit_span(unit, stride), :] = r.S[pl.ds(pl.multiple_of(row, 16), 16), lane : lane + 128].astype(F32)
+
+    for_tiles(me, tile)
+
+    def vec(row, unit, count):
+        r.E[unit : unit + count, :] = r.VS[row : row + count, :]
+
+    vec_spots(me, vec)
+    r.tail[...] = r.E[3099:3123, :]
+    up = rdma(r.tail, r.hp, r.hsem2.at[0], r.hsem2.at[1], me.next)
+    down = rdma(r.E.at[0:24], r.hn, r.hsem2.at[2], r.hsem2.at[3], me.prev)
+    up.start()
+    down.start()
+    up.wait()
+    down.wait()
+    r.E[24:48, :] += r.hp[...]
+    r.E[3075:3099, :] += r.hn[...]
+
+
+SPOTS = ((0, 16), (24592, 24608), (32800, 32824), (65592, 65624), (98392, 98400))
+
+
+def update(me, r):
+    nb = r.NB[5]
+    norms = jnp.sum(nb[0:16, :], axis=1, keepdims=True)
+    r.norms[...] = jnp.broadcast_to(norms, (16, 128))
+    r.down[...] = nb[16:24, :]
+    total = jnp.sum(norms[0:12, :], axis=0, keepdims=True)
+    clip = 1.0 / jnp.maximum(jnp.sqrt(total), 1.0)
+
+    def part(start, count):
+        grad = clip * r.E[pl.ds(24 + start, count), :]
+        at = pl.ds(start, count)
+        unit = me.d * 3075 + start + lax.broadcasted_iota(jnp.int32, (count, 128), 0)
+        plain = jnp.zeros((count, 128), jnp.bool_)
+        for lo, hi in SPOTS:
+            plain = plain | ((unit >= lo) & (unit < hi))
+        first = 0.9 * r.m[at, :] + 0.1 * grad
+        second = 0.999 * r.v[at, :] + 0.001 * grad * grad
+        direction = first / (1.0 - 0.9**10) / (jnp.sqrt(second / (1.0 - 0.999**10)) + 1e-08)
+        r.first[at, :] = first
+        r.step[at, :] = -0.001 * 0.9**12 * (direction + jnp.where(plain, 0.0, 0.05 * r.par[at, :]))
+
+    loop(48, lambda i: part(pl.multiple_of(i * 64, 8), 64))
+    part(3072, 3)
+
+
+def final(me, r):
+    gate(me.quad + me.zpeers + [me.xpeer, me.next, me.prev])
+    reduce_phase(me, r)
+    norm_exchange(me, r)
+    units_phase(me, r)
+    update(me, r)
+    reduce_drain(me, r)
+
+
+def reduce_drain(me, r):
+    arrived(r.G.at[0:6144], r.rxs)
+    arrived(r.VX.at[0:3], r.wqs)
+    arrived(r.VX, r.wxs)
+    for i in range(4):
+
+        @pl.when(me.z != i)
+        def _():
+            arrived(r.G.at[0:1536], r.rzs.at[i])
+            arrived(r.VX.at[0], r.wzs.at[i])
+
+        def visit(n, srow, size, part, row, i=i):
+            @pl.when((part == me.blk) & (me.blk != i))
+            def _():
+                arrived(rows(r.C, row, size, 32), r.qsem2.at[i * 24 + n])
+
+        Other(me, i).pieces(visit)
+
+
+FINAL_SCRATCH = dict(
+    XR=pltpu.VMEM((4, 1536, 256), BF),
+    ZR=pltpu.VMEM((4, 1536, 256), BF),
+    C=pltpu.VMEM((1536, 256), BF),
+    S=pltpu.VMEM((1536, 256), BF),
+    E=pltpu.VMEM((3128, 128), F32),
+    VX=pltpu.VMEM((4, 32, 128), F32),
+    VZ=pltpu.VMEM((4, 32, 128), F32),
+    VT=pltpu.VMEM((4, 32, 128), F32),
+    VS=pltpu.VMEM((32, 128), F32),
+    NB=pltpu.VMEM((6, 24, 128), F32),
+    NR=pltpu.VMEM((5, 24, 128), F32),
+    tail=pltpu.VMEM((24, 128), F32),
+    hp=pltpu.VMEM((24, 128), F32),
+    hn=pltpu.VMEM((24, 128), F32),
+    hsem2=DMA((4,)), rxs=DMA, rxr=DMA((12,)), rzs=DMA((4,)), rzr=DMA((12,)),
+    wxs=DMA, wxr=DMA((4,)), wzs=DMA((4,)), wzr=DMA((4,)), wqs=DMA, wqr=DMA((4,)),
+    qsem2=DMA((96,)), csem2=DMA, nsem=DMA((5,)), nrsem=DMA((5,)),
+)
+
+
+def k3(G, VG, par, m, v):
+    return call(
+        final,
+        ("G", "VG", "par", "m", "v"),
+        dict(step=((3075, 128), F32), first=((3075, 128), F32), norms=((16, 128), F32), down=((8, 128), F32)),
+        FINAL_SCRATCH,
+        2,
+        (G, VG, par, m, v),
+    )
+
+
+def fast_shards(pat, cot, lens, params, m, v):
+    def units(a):
+        return a.reshape(-1, LANE)
+
+    par = units(params)
+    F, XV, PA, CA = k1(par, pat[0], cot[0])
+    G, VG, act, ing = k2(lens[0], pat[0], cot[0], F, XV, PA, CA)
+    step, first, norms, down = k3(G, VG, par, units(m), units(v))
+    return act[None], ing[None], norms[:GROUPS, 0], step.reshape(-1), first.reshape(-1), down.reshape(-1)
+
+
 def solution(mesh):
-    in_specs = (
-        P("dp", "blk", None),
-        P("dp", "blk", None),
-        P("dp", None),
-        P(("dp", "blk")),
-        P(("dp", "blk")),
-        P(("dp", "blk")),
-    )
-    out_specs = (
-        P("dp", "blk", None),
-        P("dp", "blk", None),
-        P(),
-        P(("dp", "blk")),
-        P(("dp", "blk")),
-        P(),
-    )
-    return jax.shard_map(shards, mesh=mesh, in_specs=in_specs, out_specs=out_specs, check_vma=False)
+    act, flat = P("dp", "blk", None), P(("dp", "blk"))
+    specs = dict(
+        in_specs=(act, act, P("dp", None), flat, flat, flat), out_specs=(act, act, P(), flat, flat, P()), check_vma=False
+    )
+
+    def layer(patches, cotangent, image_lengths, params, first_moment, second_moment):
+        fits = (dict(mesh.shape), patches.shape, params.shape) == (dict(dp=8, blk=4), (8, 1024, D), (RAW,))
+        step = jax.shard_map(fast_shards if fits else shards, mesh=mesh, **specs)
+        return step(patches, cotangent, image_lengths, params, first_moment, second_moment)
+
+    return layer

time: 1640 us -> 425 us (0.26)
  waiting for transfers between devices: 991 us -> 0 us
  Pallas kernels: 0 us -> 417 us
  local copies, waits for them, and re-layouts: 252 us -> 6.86 us
  other arithmetic: 216 us -> 0 us
  matrix products: 117 us -> 0 us
  blocking collectives: 40 us -> 0 us
    unnamed x5 -> x0, waiting for transfers between devices: 696 us -> none
    pallas_call x0 -> x3, Pallas kernels: none -> 417 us  [the longest x2 266 us: call(): pl.pallas_call(kernel, out_shape=[jax.ShapeDtypeStruct(*o) for o in outs....]
    all_gather x2 -> x0, waiting for transfers between devices: 278 us -> none  [the longest x1 278 us: shards(): lax.all_gather(params.astype(jnp.bfloat16), ('dp', 'blk'), axis=0, tiled=...]
    all_gather x1 -> x0, other arithmetic: 149 us -> none  [shards(): lax.all_gather(params.astype(jnp.bfloat16), ('dp', 'blk'), axis=0, tiled=...]
    unnamed x120 -> x15, local copies, waits for them, and re-layouts: 153 us -> 5.42 us
    dot_general x26 -> x0, matrix products: 117 us -> none  [the longest x1 16.7 us: shards(): jnp.dot(normed_two_low, w_up, preferred_element_type=jnp.float32)]
    reduce_sum x16 -> x0, other arithmetic: 51.1 us -> none  [the longest x1 24.4 us: shards(): jnp.sum((positions[:, None] >= marks[None, :]).astype(jnp.int32), axis=1)]
    psum x1 -> x0, blocking collectives: 40 us -> none  [shards(): norms, bias_total = lax.psum((partials, grad_bias_down), ('dp', 'blk'))]
  transfers between devices with their start and end apart: 4 -> 0, of which waited for: 3 -> 0; matrix products, arithmetic and copies ran while one was open for 6% -> 0% of each run, Pallas kernels for 0% -> 0%
where the time goes in v1:
time: 425 us; the launch traced here: 424 us
  Pallas kernels  417 us (98%)
  local copies, waits for them, and re-layouts  6.86 us (2%)
    pallas_call x2, Pallas kernels, call(): pl.pallas_call(kernel, out_shape=[jax.ShapeDtypeStruct(*o) for o in outs....  266 us
    pallas_call x1, Pallas kernels, k2(): pl.pallas_call(kernel, out_shape=[jax.ShapeDtypeStruct(*o) for o in outs....  151 us

profile of v1, /device:TPU:0, one launch (start us, length us, event | category | flops | bytes accessed | tf_op | source)
XLA Modules:
  0.0 424.3 jit_solution(2699606387140401565)
XLA Ops:
  0.6 106.7 %shard_map.109 = (bf16[12288,256]{1,0:T(8,128)(2,1)}, f32[8,32,128]{2,1,0:T(8,128)}, bf16[1024,1024]{1,0:T(8,128)(2,1)}, bf16[1024,1024]{1,0:T(8,128)(2,1)}) custom-call(f32[3075,128]{1,0:T(8,128)} %bitcast.11, bf16[256,1024]{1,0:T(8,128)(2,1)} %bitcast.13, bf16[256,1024]{1,0:T(8,128)(2,1)} %bitcast.15), custom_call_target="tpu_custom_call" | custom-call | tf_op jit(solution)/shard_map/pallas_call | solution.py:629
  107.3 150.7 %shard_map.110 = (bf16[12288,256]{1,0:T(8,128)(2,1)}, f32[8,32,128]{2,1,0:T(8,128)}, bf16[256,1024]{1,0:T(8,128)(2,1)}, bf16[256,1024]{1,0:T(8,128)(2,1)}) custom-call(s32[9]{0:T(128)} %bitcast.24, bf16[256,1024]{1,0:T(8,128)(2,1)} %bitcast.14, bf16[256,1024]{1,0:T(8,128)(2,1)} %bitcast.16, bf16[12288,256]{1,0:T(8,128)(2,1)} %get-tuple-element.18.refs_3_, ...), custom_call_target="tpu_custom_call" | custom-call | tf_op jit(solution)/shard_map/pallas_call | solution.py:1045
  258.1 0.0 copy-start.3
  258.1 0.0 copy-start.2
  258.1 159.3 %shard_map.111 = (f32[3075,128]{1,0:T(8,128)}, f32[3075,128]{1,0:T(8,128)}, f32[16,128]{1,0:T(8,128)}, f32[8,128]{1,0:T(8,128)}) custom-call(bf16[12288,256]{1,0:T(8,128)(2,1)} %get-tuple-element.24.refs_0_, f32[8,32,128]{2,1,0:T(8,128)} %get-tuple-element.25.refs_1_, f32[3075,128]{1,0:T(8,128)} %bitcast.12, f32[3075,128]{1,0:T(8,128)} %bitcast.17, ...), custom_call_target="tpu_custom_call" | custom-call | tf_op jit(solution)/shard_map/pallas_call | solution.py:629
  417.5 0.0 copy-start.1
  417.5 1.4 slice_reduce_fusion
  418.9 0.0 copy-done.3
  418.9 0.8 copy.17
  419.7 0.0 copy-done.2
  419.7 0.8 copy.18
  420.5 0.0 copy-done.1
  420.5 0.0 copy-start
  420.5 1.2 copy.19
  421.8 0.7 copy-done
  422.5 0.0 copy-start.4
  422.5 1.2 copy.20
  423.7 0.0 copy-done.4
  423.7 0.6 copy.21
Async XLA Ops:
  258.1 160.8 %copy-start.3 = (bf16[256,1024]{1,0:T(8,128)(2,1)S(1)}, bf16[256,1024]{1,0:T(8,128)(2,1)}, u32[]{:S(2)}) copy-start(bf16[256,1024]{1,0:T(8,128)(2,1)} %get-tuple-element.22) | copy-start | bytes 1572868
  258.1 161.6 %copy-start.2 = (bf16[256,1024]{1,0:T(8,128)(2,1)S(1)}, bf16[256,1024]{1,0:T(8,128)(2,1)}, u32[]{:S(2)}) copy-start(bf16[256,1024]{1,0:T(8,128)(2,1)} %get-tuple-element.23) | copy-start | bytes 1572868
  417.5 3.0 copy-start.1
  420.5 2.0 copy-start
  422.5 1.2 copy-start.4

commit v2 on v0

--- a/solution.py
+++ b/solution.py
@@ -4,6 +4,8 @@
 import jax
 import jax.numpy as jnp
 from jax import lax
+from jax.experimental import pallas as pl
+from jax.experimental.pallas import tpu as pltpu
 from jax.sharding import PartitionSpec as P
 
 D = 1024
@@ -286,21 +288,1105 @@
     )
 
 
+MESH = pl.DeviceIdType.MESH
+LANE = 128
+
+
+def pick(cond, yes, no):
+    return jnp.where(cond, jnp.int32(yes), jnp.int32(no))
+
+
+def rdma(src, dst, ssem, rsem, dev):
+    return pltpu.make_async_remote_copy(src_ref=src, dst_ref=dst, send_sem=ssem, recv_sem=rsem, device_id=dev, device_id_type=MESH)
+
+
+def rows(ref, start, size, step=128):
+    return ref.at[pl.ds(pl.multiple_of(start, step), size)]
+
+
+def gate(peers):
+    sem = pltpu.get_barrier_semaphore()
+    for peer in peers:
+        pl.semaphore_signal(sem, inc=1, device_id=peer, device_id_type=MESH)
+    pl.semaphore_wait(sem, len(peers))
+
+
+class Place:
+    def __init__(self):
+        self.dp = lax.axis_index("dp")
+        self.blk = lax.axis_index("blk")
+        self.d = self.dp * 4 + self.blk
+        self.z = self.dp // 2
+        self.x = self.dp % 2
+        self.y = self.blk // 2
+        self.c = self.blk % 2
+        self.xpeer = (self.z * 2 + 1 - self.x, self.blk)
+        self.zs = [lax.rem(self.z + k, 4) for k in (1, 3, 2)]
+        self.zpeers = [(zz * 2 + self.x, self.blk) for zz in self.zs]
+        self.quad = [(self.dp, lax.rem(self.blk + k, 4)) for k in (1, 2, 3)]
+        up = lax.rem(self.d + 1, 32)
+        down = lax.rem(self.d + 31, 32)
+        self.above = (self.dp + 2, self.blk)
+        self.below = (self.dp - 2, self.blk)
+        self.others = self.zpeers + [(zz * 2 + 1 - self.x, self.blk) for zz in self.zs]
+        self.next = (up // 4, up % 4)
+        self.prev = (down // 4, down % 4)
+        d = self.d
+        self.is_qkv = d < 8
+        self.is_out = (d == 8) | (d == 9)
+        self.is_mix_out = d == 10
+        self.is_up = (d >= 11) & (d < 21)
+        self.is_mix_down = d == 21
+        self.is_down = d >= 22
+        self.is_seg = self.is_out | self.is_down
+        self.is_mix = self.is_mix_out | self.is_mix_down
+        self.base = pick(d < 8, 16, pick(d < 11, 32, pick(d < 21, 56, 88))) - 3 * d
+        self.seg0 = pick(d < 11, 3 * (d - 8), jnp.maximum(3 * (d - 21) - 1, 0))
+        self.mix_up = pick(self.is_mix_out, 2074, -7)
+        self.mix_seg = pick(self.is_mix_out, 2, 1049)
+
+    def seg_home(self, n):
+        seg = self.seg0 + n // 4
+        panel = n % 4
+        out_row = 3072 + 256 * panel + 128 * (seg % 2)
+        down_row = 8192 + 1024 * panel + 128 * (seg // 4)
+        low = self.d < 11
+        return pick(low, seg // 2, seg % 4), pick(low, out_row, down_row)
+
+    def block_home(self, n):
+        part, row = self.seg_home(n)
+        return pick(self.is_qkv, n // 3, part), pick(self.is_qkv, (n % 3) * 1024 + 128 * self.d, row)
+
+    def up_home(self, n):
+        start = pick(self.is_up, 32 + 96 * (self.d - 11), pick(self.is_mix_out, 0, 992))
+        return n // 4, 4096 + 1024 * (n % 4) + start
+
+
+def chunk_row(q, k):
+    first = (k // 4) * 1024 + 512 * q + 128 * (k % 4)
+    turn = 3 * (q - 2) + k // 4
+    panel = k % 4
+    other = pick(
+        turn < 2,
+        3072 + 256 * panel + 128 * turn,
+        pick(turn < 10, 4096 + 1024 * panel + 128 * (turn - 2), 8192 + 1024 * panel + 128 * (turn - 10)),
+    )
+    return pick(q < 2, first, other)
+
+
+def loop(count, body):
+    def step(i, carry):
+        body(i)
+        return carry
+
+    lax.fori_loop(0, count, step, 0)
+
+
+def unit_span(start, stride):
+    return pl.ds(start, 16, stride=stride)
+
+
+def for_tiles(me, visit):
+    e0 = 24 + me.base
+
+    @pl.when(me.is_qkv)
+    def _():
+        def body(rb):
+            for ct in range(24):
+                n = ((ct % 8) // 2) * 3 + ct // 8
+                visit(e0 + 384 * rb + ct, 24, n * 128 + 16 * rb, 128 * (ct % 2))
+
+        loop(8, body)
+
+    @pl.when(me.is_up)
+    def _():
+        def body(rb):
+            for ct in range(32):
+                n = (ct % 4) * 4 + ct // 8
+                visit(e0 + 512 * rb + ct, 32, n * 96 + 16 * rb, 128 * ((ct // 4) % 2))
+
+        loop(6, body)
+
+    def segs(count, first):
+        def body(i):
+            for ct in range(8):
+                visit(first + 128 * i + ct, 8, ((i // 8) * 4 + ct // 2) * 128 + 16 * (i % 8), 128 * (ct % 2))
+
+        loop(count, body)
+
+    @pl.when(me.is_seg)
+    def _():
+        segs(24, e0)
+
+    @pl.when(me.is_mix)
+    def _():
+        segs(16, 24 + me.mix_seg)
+
+        def body(rb):
+            for ct in range(32):
+                n = (ct % 4) * 4 + ct // 8
+                visit(24 + me.mix_up + 512 * rb + ct, 32, 1024 + n * 32 + 16 * rb, 128 * ((ct // 4) % 2))
+
+        loop(2, body)
+
+
+def for_pieces(me, visit):
+    @pl.when(me.is_qkv | me.is_seg)
+    def _():
+        def body(n):
+            part, row = me.block_home(n)
+            visit(n, n * 128, 128, part, row, 128)
+
+        loop(12, body)
+
+    @pl.when(me.is_up)
+    def _():
+        def body(n):
+            part, row = me.up_home(n)
+            visit(n, n * 96, 96, part, row, 32)
+
+        loop(16, body)
+
+    @pl.when(me.is_mix)
+    def _():
+        def body(n):
+            part, row = me.seg_home(n)
+            visit(n, n * 128, 128, part, row, 128)
+
+        loop(8, body)
+
+        def body_up(n):
+            part, row = me.up_home(n)
+            visit(8 + n, 1024 + n * 32, 32, part, row, 32)
+
+        loop(16, body_up)
+
+
+def vec_spots(me, visit):
+    for cond, row, unit, count in (
+        (me.d == 0, 0, 0, 16),
+        (me.d == 7, 0, 3067, 8),
+        (me.d == 8, 0, 0, 8),
+        (me.d == 10, 8, 2050, 24),
+        (me.d == 21, 0, 1017, 32),
+        (me.d == 31, 0, 3067, 8),
+    ):
+
+        @pl.when(cond)
+        def _(row=row, unit=unit, count=count):
+            visit(row, 24 + unit, count)
+
+
+BF, F32 = jnp.bfloat16, jnp.float32
+EPS = 1e-06
+OUT0, UP0, DOWN0 = 3072, 4096, 8192
+
+
+def dot(a, b):
+    return lax.dot_general(a, b, (((1,), (0,)), ((), ())), preferred_element_type=F32)
+
+
+def dot_nt(a, b):
+    return lax.dot_general(a, b, (((1,), (1,)), ((), ())), preferred_element_type=F32)
+
+
+def dot_tn(a, b):
+    return lax.dot_general(a, b, (((0,), (0,)), ((), ())), preferred_element_type=F32)
+
+
+def block_of(i):
+    return pl.ds(pl.multiple_of(i * 256, 256), 256)
+
+
+def wide(r, q, first, count=8):
+    return jnp.concatenate([r.XV[q, first + i : first + i + 1, :] for i in range(count)], axis=1)
+
+
+def narrow(r, q, first):
+    return jnp.concatenate([r.XV[q, pl.ds(first + i, 1), :] for i in range(2)], axis=1)
+
+
+def put_vec(r, q, first, row, add=False):
+    for i in range(row.shape[1] // 128):
+        part = row[:, i * 128 : i * 128 + 128]
+        if add:
+            part = part + r.VG[q, first + i : first + i + 1, :]
+        r.VG[q, first + i : first + i + 1, :] = part
+
+
+def normalize(x):
+    mean = jnp.mean(x, axis=-1, keepdims=True)
+    cen = x - mean
+    var = jnp.mean(cen * cen, axis=-1, keepdims=True)
+    scale = lax.rsqrt(var + EPS)
+    return cen * scale, scale
+
+
+def norm_back(dy, xhat, scale, gain):
+    t = dy * gain
+    return scale * (t - jnp.mean(t, axis=-1, keepdims=True) - xhat * jnp.mean(t * xhat, axis=-1, keepdims=True))
+
+
+def labels_at(r, at):
+    total = jnp.zeros_like(at)
+    bound = 0
+    for k in range(9):
+        bound = bound + r.lens[k]
+        total = total + (at >= bound).astype(jnp.int32)
+    return total
+
+
+def lane_mask(h):
+    lane = lax.broadcasted_iota(jnp.int32, (1, 128), 1)
+    return ((lane // 64) == h).astype(BF)
+
+
+def crow(q, k):
+    return pick(q < 2, 128 * k, 384 * (k % 4) + 128 * (k // 4))
+
+
+class Other(Place):
+    def __init__(self, me, i):
+        d = me.dp * 4 + i
+        self.d, self.blk, self.dp = d, i, me.dp
+        self.is_qkv = d < 8
+        self.is_out = (d == 8) | (d == 9)
+        self.is_mix_out = d == 10
+        self.is_up = (d >= 11) & (d < 21)
+        self.is_mix_down = d == 21
+        self.is_down = d >= 22
+        self.is_seg = self.is_out | self.is_down
+        self.is_mix = self.is_mix_out | self.is_mix_down
+        self.seg0 = pick(d < 11, 3 * (d - 8), jnp.maximum(3 * (d - 21) - 1, 0))
+
+    def seg_spot(self, n):
+        seg = self.seg0 + n // 4
+        low = self.d < 11
+        turn = pick(low, seg % 2, 10 + seg // 4 - 3 * (self.dp - 2))
+        return pick(low, seg // 2, seg % 4), 384 * (n % 4) + 128 * turn
+
+    def block_spot(self, n):
+        part, row = self.seg_spot(n)
+        return pick(self.is_qkv, n // 3, part), pick(self.is_qkv, (n % 3) * 512 + 128 * (self.d % 4), row)
+
+    def up_spot(self, n):
+        start = pick(self.is_up, 32 + 96 * (self.d - 11), pick(self.is_mix_out, 0, 992))
+        return n // 4, 384 * (n % 4) + 256 + start - 384 * (self.dp - 2)
+
+    def pieces(self, visit):
+        @pl.when(self.is_qkv | self.is_seg)
+        def _():
+            loop(12, lambda n: visit(n, n * 128, 128, *self.block_spot(n)))
+
+        @pl.when(self.is_up)
+        def _():
+            loop(16, lambda n: visit(n, n * 96, 96, *self.up_spot(n)))
+
+        @pl.when(self.is_mix)
+        def _():
+            loop(8, lambda n: visit(n, n * 128, 128, *self.seg_spot(n)))
+            loop(16, lambda n: visit(8 + n, 1024 + n * 32, 32, *self.up_spot(n)))
+
+
+def arrived(ref, sem):
+    pltpu.make_async_copy(ref, ref, sem).wait()
+
+
+def squares(x):
+    s = jnp.sum(x * x, axis=0, keepdims=True)
+    return s[:, :128] + s[:, 128:] if x.shape[1] == 256 else s
+
+
+def reduce_vectors(me, r):
+    for zz in range(4):
+        arrived(r.VX.at[0], r.wxr.at[zz])
+        r.VX[zz] = r.VX[zz] + r.VG[zz * 2 + me.x]
+
+        @pl.when(me.z != zz)
+        def _():
+            rdma(r.VX.at[zz], r.VZ.at[me.z], r.wzs.at[zz], r.wzr.at[me.z], (zz * 2 + me.x, me.blk)).start()
+
+    total = r.VX[me.z]
+    for zz in me.zs:
+        arrived(r.VZ.at[0], r.wzr.at[zz])
+        total = total + r.VZ[zz]
+    r.VT[me.blk] = total
+    outs = [rdma(r.VT.at[me.blk], r.VT.at[me.blk], r.wqs, r.wqr.at[me.blk], peer) for peer in me.quad]
+    for o in outs:
+        o.start()
+    for k in (1, 2, 3):
+        arrived(r.VT.at[0], r.wqr.at[lax.rem(me.blk + k, 4)])
+    r.VS[...] = r.VT[0] + r.VT[1] + r.VT[2] + r.VT[3]
+
+
+def norm_exchange(me, r):
+    zx = [(me.z + 1 - 2 * (me.z % 2)), lax.rem(me.z + 2, 4)]
+    peers = [(me.dp, me.y * 2 + 1 - me.c), (me.dp, (1 - me.y) * 2 + me.c), me.xpeer] + [(z * 2 + me.x, me.blk) for z in zx]
+    for n, peer in enumerate(peers):
+        cp = rdma(r.NB.at[n], r.NR.at[n], r.nsem.at[n], r.nrsem.at[n], peer)
+        cp.start()
+        cp.wait()
+        r.NB[n + 1] = r.NB[n] + r.NR[n]
+
+
+def by_z(me, values):
+    out = jnp.int32(values[0])
+    for n in (1, 2, 3):
+        out = pick(me.z == n, values[n], out)
+    return out
+
+
+GATHER_ORDER = (
+    (0, 1, 2, 3, 4, 5, 6, 7, 8, 9, 10, 11),
+    (3, 0, 1, 2, 4, 5, 6, 7, 8, 9, 10, 11),
+    (6, 7, 0, 1, 2, 9, 3, 10, 4, 11, 8, 5),
+    (9, 10, 11, 0, 1, 2, 6, 3, 7, 4, 8, 5),
+)
+REDUCE_ORDER = (
+    (9, 10, 11, 6, 7, 8, 3, 4, 5, 12, 12, 12, 12, 12),
+    (12, 9, 10, 11, 6, 7, 8, 12, 12, 12, 12, 0, 1, 2),
+    (12, 12, 9, 10, 11, 12, 12, 3, 4, 5, 0, 1, 2, 12),
+    (12, 12, 12, 6, 7, 8, 3, 4, 5, 0, 1, 2, 12, 12),
+)
+
+
+def prepare(me, r):
+    r.tail[...] = r.par[3051:3075, :]
+    up = rdma(r.tail, r.hp, r.hsem.at[0], r.hsem.at[1], me.next)
+    down = rdma(r.par.at[0:24], r.hn, r.hsem.at[2], r.hsem.at[3], me.prev)
+    up.start()
+    down.start()
+
+    def put(i):
+        r.E[pl.ds(pl.multiple_of(24 + 64 * i, 8), 64), :] = r.par[pl.ds(pl.multiple_of(64 * i, 8), 64), :]
+
+    loop(48, put)
+    r.E[3096:3099, :] = r.par[3072:3075, :]
+    r.VS[...] = jnp.zeros_like(r.VS)
+
+    def vec(row, unit, count):
+        r.VS[row : row + count, :] = r.E[unit : unit + count, :].astype(BF).astype(F32)
+
+    vec_spots(me, vec)
+    vq = [rdma(r.VS, r.VQ.at[me.blk], r.vsem.at[0], r.vsem.at[1], peer) for peer in me.quad]
+    for v in vq:
+        v.start()
+    r.VQ[me.blk] = r.VS[...]
+    up.wait()
+    down.wait()
+    r.E[0:24, :] = r.hp[...]
+    r.E[3099:3123, :] = r.hn[...]
+
+    def tile(unit, stride, row, lane):
+        r.S[pl.ds(pl.multiple_of(row, 16), 16), lane : lane + 128] = r.E[unit_span(unit, stride), :].astype(BF)
+
+    for_tiles(me, tile)
+
+    def visit(i, srow, size, part, frow, step):
+        src, dst = rows(r.S, srow, size, 32), rows(r.F, frow, size, step)
+
+        @pl.when(part != me.blk)
+        def _():
+            rdma(src, dst, r.qsem.at[i], r.csem, (me.dp, part)).start()
+
+        @pl.when(part == me.blk)
+        def _():
+            pltpu.make_async_copy(src, dst, r.csem).start()
+
+    for_pieces(me, visit)
+    arrived(r.VQ.at[0:3], r.vsem.at[0])
+    arrived(r.VQ.at[0:3], r.vsem.at[1])
+    r.XV[me.dp] = r.VQ[0] + r.VQ[1] + r.VQ[2] + r.VQ[3]
+    for peer in me.others + [me.xpeer]:
+        rdma(r.XV.at[me.dp], r.XV.at[me.dp], r.vxs, r.vxr.at[me.dp], peer).start()
+    arrived(r.F.at[0:1536], r.csem)
+
+
+def prepare_drain(me, r):
+    def visit(i, srow, size, part, frow, step):
+        @pl.when(part != me.blk)
+        def _():
+            arrived(rows(r.S, srow, size, 32), r.qsem.at[i])
+
+    for_pieces(me, visit)
+    arrived(r.XV.at[0:7], r.vxs)
+
+
+def gather_step(me, r, s):
+    e = by_z(me, [order[s] for order in GATHER_ORDER])
+    zz, g = e // 3, e % 3
+
+    @pl.when(zz != me.z)
+    def _():
+        arrived(r.F.at[0:512], r.zr.at[e])
+
+    def block(i):
+        return rows(r.F, chunk_row(zz * 2 + me.x, g * 4 + i), 128)
+
+    @pl.when((zz <= me.z) & (me.z < 3))
+    def _():
+        for i in range(4):
+            rdma(block(i), block(i), r.zsu.at[zz], r.zr.at[e], me.above).start()
+
+    @pl.when((zz >= me.z) & (me.z > 0))
+    def _():
+        for i in range(4):
+            rdma(block(i), block(i), r.zsd.at[zz], r.zr.at[e], me.below).start()
+
+    for i in range(4):
+        rdma(block(i), block(i), r.xs, r.xr.at[e], me.xpeer).start()
+
+
+def gathered(me, r, entries):
+    for e in entries:
+        arrived(r.F.at[0:512], r.xr.at[e])
+
+
+def gather_drain(me, r):
+    arrived(r.F.at[0:6144], r.xs)
+    for zz in range(4):
+        @pl.when((zz <= me.z) & (me.z < 3))
+        def _():
+            arrived(r.F.at[0:1536], r.zsu.at[zz])
+
+        @pl.when((zz >= me.z) & (me.z > 0))
+        def _():
+            arrived(r.F.at[0:1536], r.zsd.at[zz])
+
+
+def share_rows(me, r):
+    mine = block_of(me.blk)
+    for n, (src, dst) in enumerate(((r.pat, r.PA), (r.cot, r.CA))):
+        for peer in me.quad:
+            rdma(src, dst.at[mine], r.asem.at[2 * n], r.asem.at[2 * n + 1], peer).start()
+        dst[mine, :] = src[...]
+
+
+def nothing(n):
+    pass
+
+
+def quad_sum(me, r, make, sems, finish, slot, buf=None, idle=nothing):
+    y, c = me.y, me.c
+    sib, yp = (me.dp, y * 2 + 1 - c), (me.dp, (1 - y) * 2 + c)
+    far_sib, far, near_sib, own = (1 - y) * 2 + 1 - c, (1 - y) * 2 + c, y * 2 + 1 - c, me.blk
+    ssem, rsem = sems
+
+    def copy(src, dst, n, dev):
+        return rdma(src, dst, ssem.at[n], rsem.at[n], dev)
+
+    def at(dev, i):
+        return pl.ds(pl.multiple_of(dev * 256 + 64 * i, 64), 64)
+
+    make(far_sib)
+    a = copy(r.PB.at[block_of(far_sib)], r.RB.at[0], 0, sib)
+    a.start()
+    make(far)
+    a.wait_recv()
+    over = []
+    for i in range(4):
+        lo = pl.ds(64 * i, 64)
+        r.RB[3, lo, :] = (r.PB[at(far, i), :].astype(F32) + r.RB[0, lo, :].astype(F32)).astype(BF)
+        over.append(copy(r.RB.at[3, lo], r.RB.at[slot, lo], 2 + i, yp))
+        over[i].start()
+    make(near_sib)
+    d = copy(r.PB.at[block_of(near_sib)], r.RB.at[1], 1, sib)
+    d.start()
+    make(own)
+    idle(0)
+    d.wait_recv()
+    out, near, on = [], [], []
+    for i in range(4):
+        over[i].wait_recv()
+        lo = slice(64 * i, 64 * i + 64)
+        finish(lo, r.PB[at(own, i), :].astype(F32) + r.RB[1, lo, :].astype(F32) + r.RB[slot, lo, :].astype(F32))
+        if buf is not None:
+            part, passed = buf.at[at(own, i)], buf.at[at(far, i)]
+            out.append(copy(part, part, 6 + i, yp))
+            near.append(copy(part, part, 10 + i, sib))
+            on.append(copy(passed, passed, 14 + i, sib))
+            out[i].start()
+            near[i].start()
+    idle(1)
+    for i in range(len(out)):
+        out[i].wait_recv()
+        on[i].start()
+    for cp in near + on:
+        cp.wait()
+    for cp in [a, d] + over + out:
+        cp.wait_send()
+
+
+def first_norm(me, r):
+    arrived(r.PA.at[0:768], r.asem.at[1])
+    for peer in range(1, 8):
+        arrived(r.XV.at[0], r.vxr.at[lax.rem(me.dp + peer, 8)])
+    gain, shift = wide(r, 0, 0), wide(r, 0, 8)
+
+    def ln(i):
+        at = pl.ds(pl.multiple_of(i * 64, 64), 64)
+        xhat, _ = normalize(r.PA[at, :].astype(F32))
+        r.PA[at, :] = (xhat * gain + shift).astype(BF)
+
+    loop(16, ln)
+
+
+def attention(me, r, idle):
+    bias = [narrow(r, 1, 2 * me.blk), None, narrow(r, 2, 2 * me.blk)]
+
+    def proj(i):
+        at = block_of(i)
+        for j in range(3):
+            out = dot(r.PA[at, :], r.F[j * 1024 : j * 1024 + 1024, :])
+            if bias[j] is not None:
+                out = out + bias[j]
+            r.QKV[j, at, :] = out.astype(BF)
+
+    loop(4, proj)
+    idle(0)
+    key_labels = labels_at(r, lax.broadcasted_iota(jnp.int32, (1, 1024), 1))
+
+    def attend(i):
+        at = block_of(i)
+        row_labels = labels_at(r, lax.broadcasted_iota(jnp.int32, (256, 1), 0) + i * 256)
+        allowed = row_labels == key_labels
+        for t in range(2):
+            lanes = slice(128 * t, 128 * t + 128)
+            q = r.QKV[0, at, lanes]
+            k = r.QKV[1, :, lanes]
+            v = r.QKV[2, :, lanes]
+            out = jnp.zeros((256, 128), F32)
+            for h in range(2):
+                m = lane_mask(h)
+                s = jnp.where(allowed, dot_nt(q * m, k) * 0.125, -1e30)
+                w = jnp.exp(s - jnp.max(s, axis=-1, keepdims=True))
+                p = (w * (1.0 / jnp.sum(w, axis=-1, keepdims=True))).astype(BF)
+                r.P[2 * t + h, at, :] = p
+                out = out + dot(p, v * m)
+            r.AT[at, lanes] = out.astype(BF)
+
+    loop(2, attend)
+    idle(1)
+    loop(2, lambda i: attend(i + 2))
+
+
+def second_norm(me, r, idle):
+    def term(i):
+        at = block_of(i)
+        for p in range(4):
+            r.PB[at, 256 * p : 256 * p + 256] = dot(r.AT[at, :], r.F[OUT0 + 256 * p : OUT0 + 256 * p + 256, :]).astype(BF)
+
+    bias_out = wide(r, 2, 8)
+    gain, shift = wide(r, 2, 16), wide(r, 2, 24)
+
+    def finish(lo, total):
+        x = r.pat[lo, :].astype(F32) + (total + bias_out)
+        r.MID[lo, :] = x
+        xhat, _ = normalize(x)
+        r.NT[pl.ds(pl.multiple_of(me.blk * 256 + lo.start, 64), 64), :] = (xhat * gain + shift).astype(BF)
+
+    quad_sum(me, r, term, (r.s1s, r.s1r), finish, 2, r.NT, idle)
+
+
+def hidden(me, r):
+    biases = [jnp.concatenate([r.XV[5, pl.ds(4 * (2 * p + i) + me.blk, 1), :] for i in range(2)], axis=1) for p in range(4)]
+
+    def up(i):
+        at = pl.ds(pl.multiple_of(i * 128, 128), 128)
+        for p in range(4):
+            h = dot(r.NT[at, :], r.F[UP0 + 1024 * p : UP0 + 1024 * p + 1024, :]) + biases[p]
+            phi = 0.5 + 0.5 * lax.erf(h * 0.7071067811865476)
+            lanes = slice(256 * p, 256 * p + 256)
+            r.AC[at, lanes] = (h * phi).astype(BF)
+            r.GP[at, lanes] = (phi + h * (jnp.exp(-0.5 * h * h) * 0.3989422804014327)).astype(BF)
+
+    loop(8, up)
+
+
+def hidden_grad(me, r):
+    arrived(r.CA.at[0:768], r.asem.at[3])
+
+    def body(i):
+        at = block_of(i)
+        for p in range(4):
+            lanes = slice(256 * p, 256 * p + 256)
+            acc = jnp.zeros((256, 256), F32)
+            for k in range(4):
+                down = r.F[DOWN0 + 1024 * k + 256 * p : DOWN0 + 1024 * k + 256 * p + 256, :]
+                acc = acc + dot_nt(r.CA[at, 256 * k : 256 * k + 256], down)
+            r.GH[at, lanes] = (acc * r.GP[at, lanes].astype(F32)).astype(BF)
+
+    loop(4, body)
+
+
+def hidden_sums(me, r):
+    for p in range(4):
+        sums = jnp.sum(r.GH[:, 256 * p : 256 * p + 256].astype(F32), axis=0, keepdims=True)
+        for i in range(2):
+            r.VG[5, pl.ds(4 * (2 * p + i) + me.blk, 1), :] = sums[:, 128 * i : 128 * i + 128]
+    put_vec(r, 7, 0, jnp.sum(r.cot[...].astype(F32), axis=0, keepdims=True))
+
+
+def weight_grad(r, left, right, base, height):
+    def body(i):
+        cols = pl.ds(pl.multiple_of(i * 256, 256), 256)
+        lt = left[:, cols].T
+        for p in range(right.shape[1] // 256):
+            out = dot(lt, right[:, 256 * p : 256 * p + 256])
+            r.G[pl.ds(pl.multiple_of(base + p * height + i * 256, 256), 256), :] = out.astype(BF)
+
+    loop(height // 256, body)
+
+
+def middle_grad(me, r, idle):
+    def term(i):
+        at = block_of(i)
+        for n in range(4):
+            acc = jnp.zeros((256, 256), F32)
+            for p in range(4):
+                up = r.F[UP0 + 1024 * p + 256 * n : UP0 + 1024 * p + 256 * n + 256, :]
+                acc = acc + dot_nt(r.GH[at, 256 * p : 256 * p + 256], up)
+            r.PB[at, 256 * n : 256 * n + 256] = acc.astype(BF)
+
+    gain = wide(r, 2, 16)
+    sums = [jnp.zeros((1, 1024), F32)] * 3
+
+    def finish(lo, dy):
+        xhat, scale = normalize(r.MID[lo, :])
+        gm = r.cot[lo, :].astype(F32) + norm_back(dy, xhat, scale, gain)
+        r.GMID[lo, :] = gm
+        low = gm.astype(BF)
+        r.NT[pl.ds(pl.multiple_of(me.blk * 256 + lo.start, 64), 64), :] = low
+        for n, term_of in enumerate((low.astype(F32), dy * xhat, dy)):
+            sums[n] = sums[n] + jnp.sum(term_of, axis=0, keepdims=True)
+
+    quad_sum(me, r, term, (r.s2s, r.s2r), finish, 4, r.NT, idle)
+    for n in range(3):
+        put_vec(r, 2, 8 + 8 * n, sums[n])
+
+
+def attended_grad(me, r):
+    def body(i):
+        at = block_of(i)
+        acc = jnp.zeros((256, 256), F32)
+        for p in range(4):
+            acc = acc + dot_nt(r.NT[at, 256 * p : 256 * p + 256], r.F[OUT0 + 256 * p : OUT0 + 256 * p + 256, :])
+        r.GP[at, 768:1024] = acc.astype(BF)
+
+    loop(4, body)
+
+
+def attention_grad(me, r, idle):
+    r.KV[...] = jnp.zeros_like(r.KV)
+
+    def attend(i):
+        at = block_of(i)
+        for t in range(2):
+            lanes = slice(128 * t, 128 * t + 128)
+            q = r.QKV[0, at, lanes]
+            k = r.QKV[1, :, lanes]
+            v = r.QKV[2, :, lanes]
+            da = r.GP[at, 768 + 128 * t : 896 + 128 * t]
+            dq = jnp.zeros((256, 128), F32)
+            for h in range(2):
+                m = lane_mask(h)
+                p = r.P[2 * t + h, at, :]
+                pf = p.astype(F32)
+                dp = dot_nt(da * m, v)
+                delta = jnp.sum(pf * dp, axis=-1, keepdims=True)
+                ds = (pf * (dp - delta) * 0.125).astype(BF)
+                dq = dq + dot(ds, k * m)
+                r.KV[0, :, lanes] += dot_tn(ds, q * m)
+                r.KV[1, :, lanes] += dot_tn(p, da * m)
+            r.GP[at, lanes] = dq.astype(BF)
+
+    loop(2, attend)
+    idle(0)
+    loop(2, lambda i: attend(i + 2))
+    r.GP[:, 256:512] = r.KV[0].astype(BF)
+    r.GP[:, 512:768] = r.KV[1].astype(BF)
+
+
+def projection_sums(me, r):
+    for j, q in ((0, 1), (2, 2)):
+        sums = jnp.sum(r.GP[:, 256 * j : 256 * j + 256].astype(F32), axis=0, keepdims=True)
+        for i in range(2):
+            r.VG[q, pl.ds(2 * me.blk + i, 1), :] = sums[:, 128 * i : 128 * i + 128]
+
+
+def projection_grad(me, r):
+    def body(i):
+        cols = pl.ds(pl.multiple_of(i * 256, 256), 256)
+        lt = r.PA[:, cols].T
+        for j in range(3):
+            r.G[pl.ds(pl.multiple_of(j * 1024 + i * 256, 256), 256), :] = dot(lt, r.GP[:, 256 * j : 256 * j + 256]).astype(BF)
+
+    loop(4, body)
+
+
+def input_grad(me, r, idle):
+    def term(i):
+        at = block_of(i)
+        for n in range(4):
+            acc = jnp.zeros((256, 256), F32)
+            for j in range(3):
+                acc = acc + dot_nt(r.GP[at, 256 * j : 256 * j + 256], r.F[1024 * j + 256 * n : 1024 * j + 256 * n + 256, :])
+            r.PB[at, 256 * n : 256 * n + 256] = acc.astype(BF)
+
+    gain = wide(r, 0, 0)
+    sums = [jnp.zeros((1, 1024), F32)] * 2
+
+    def finish(lo, dy):
+        xhat, scale = normalize(r.pat[lo, :].astype(F32))
+        r.ing[lo, :] = (r.GMID[lo, :] + norm_back(dy, xhat, scale, gain)).astype(BF)
+        for n, term_of in enumerate((dy * xhat, dy)):
+            sums[n] = sums[n] + jnp.sum(term_of, axis=0, keepdims=True)
+
+    quad_sum(me, r, term, (r.s3s, r.s3r), finish, 2, None, idle)
+    for n in range(2):
+        put_vec(r, 0, 8 * n, sums[n])
+
+
+def layer_out(me, r, idle):
+    def term(i):
+        at = block_of(i)
+        for p in range(4):
+            r.PB[at, 256 * p : 256 * p + 256] = dot(r.AC[at, :], r.F[DOWN0 + 1024 * p : DOWN0 + 1024 * p + 1024, :]).astype(BF)
+
+    bias_down = wide(r, 7, 0)
+
+    def finish(lo, total):
+        r.act[lo, :] = (r.MID[lo, :] + (total + bias_down)).astype(BF)
+
+    quad_sum(me, r, term, (r.s4s, r.s4r), finish, 4, None, idle)
+
+
+def reduce_send(me, r, entries):
+    for e in entries:
+        zz, g = e // 3, e % 3
+        q = zz * 2 + 1 - me.x
+
+        def body(i, q=q, zz=zz, g=g, e=e):
+            k = g * 4 + i
+            rdma(rows(r.G, chunk_row(q, k), 128), rows(r.XR.at[zz], crow(q, k), 128), r.rxs, r.rxr.at[e], me.xpeer).start()
+
+        loop(4, body)
+
+
+def reduce_step(me, r, s):
+    e = by_z(me, [order[s] for order in REDUCE_ORDER])
+
+    @pl.when(e < 12)
+    def _():
+        zz, g = e // 3, e % 3
+        q = zz * 2 + me.x
+        down = zz < me.z
+        arrived(r.G.at[0:512], r.rxr.at[e])
+
+        @pl.when((me.z > 0) & (me.z < 3))
+        def _():
+            arrived(r.G.at[0:512], r.rzr.at[e])
+
+        def body(i):
+            k = g * 4 + i
+            src, at = pl.ds(pl.multiple_of(chunk_row(q, k), 128), 128), pl.ds(pl.multiple_of(crow(q, k), 128), 128)
+            total = r.G[src, :].astype(F32) + r.XR[zz, at, :].astype(F32) + r.ZR[zz, at, :].astype(F32)
+            r.XR[zz, at, :] = total.astype(BF)
+            sent = rows(r.XR.at[zz], crow(q, k), 128)
+
+            @pl.when(down)
+            def _():
+                rdma(sent, rows(r.ZR.at[zz], crow(q, k), 128), r.rzs.at[zz], r.rzr.at[e], me.below).start()
+
+            @pl.when(jnp.logical_not(down))
+            def _():
+                last = zz == me.z + 1
+                slot, sem = pick(last, 4, zz), pick(last, 12 + g, e)
+                rdma(sent, rows(r.ZR.at[slot], crow(q, k), 128), r.rzs.at[zz], r.rzr.at[sem], me.above).start()
+
+        loop(4, body)
+
+
+def reduce_last(me, r):
+    first_tensor = pick(me.dp < 2, 2, pick(me.dp == 2, 4, pick(me.dp < 6, 8, 10)))
+    for g in range(3):
+        e = me.z * 3 + g
+        arrived(r.G.at[0:512], r.rxr.at[e])
+
+        @pl.when(me.z < 3)
+        def _():
+            arrived(r.G.at[0:512], r.rzr.at[e])
+
+        @pl.when(me.z > 0)
+        def _():
+            arrived(r.G.at[0:512], r.rzr.at[12 + g])
+
+        part = jnp.zeros((1, 128), F32)
+        for i in range(4):
+            k = g * 4 + i
+            src, at = pl.ds(pl.multiple_of(chunk_row(me.dp, k), 128), 128), pl.ds(pl.multiple_of(crow(me.dp, k), 128), 128)
+            total = r.G[src, :].astype(F32) + r.XR[me.z, at, :].astype(F32)
+            total = total + (r.ZR[me.z, at, :].astype(F32) + r.ZR[4, at, :].astype(F32))
+            part = part + squares(total)
+            r.XR[me.z, at, :] = total.astype(BF)
+        tensor = first_tensor
+        if g == 2:
+            tensor = pick(me.dp == 2, 8, tensor)
+        if g >= 1:
+            tensor = pick(me.dp == 5, 10, tensor)
+        r.NB[0, pl.ds(tensor, 1), :] += part
+    for i in range(4):
+        def visit(n, srow, size, part, row, i=i):
+            src, dst = rows(r.XR.at[me.z], row, size, 32), rows(r.S, srow, size, 32)
+
+            @pl.when((part == me.blk) & (me.blk != i))
+            def _():
+                rdma(src, dst, r.qsem2.at[i * 24 + n], r.csem2, (me.dp, i)).start()
+
+            @pl.when((part == me.blk) & (me.blk == i))
+            def _():
+                pltpu.make_async_copy(src, dst, r.csem2).start()
+
+        Other(me, i).pieces(visit)
+
+
+def vector_squares(me, r):
+    for q, tensors in ((0, (0, 1, None, None)), (1, (3, None, None, None)), (2, (3, 5, 6, 7)), (5, (9, 9, 9, 9)), (7, (11, None, None, None))):
+        @pl.when((me.dp == q) & (me.blk == 0))
+        def _(q=q, tensors=tensors):
+            for g, tensor in enumerate(tensors):
+                if tensor is not None:
+                    r.NB[0, tensor : tensor + 1, :] += squares(r.VS[8 * g : 8 * g + 8, :])
+            if q == 7:
+                r.NB[0, 16:24, :] = r.VS[0:8, :]
+
+
+def reduce_drain(me, r):
+    arrived(r.G.at[0:6144], r.rxs)
+    arrived(r.VX.at[0:3], r.wqs)
+    arrived(r.VX, r.wxs)
+    for i in range(4):
+        @pl.when(me.z != i)
+        def _(i=i):
+            arrived(r.G.at[0:1536], r.rzs.at[i])
+            arrived(r.VX.at[0], r.wzs.at[i])
+
+        def visit(n, srow, size, part, row, i=i):
+            @pl.when((part == me.blk) & (me.blk != i))
+            def _():
+                arrived(rows(r.XR.at[me.z], row, size, 32), r.qsem2.at[i * 24 + n])
+
+        Other(me, i).pieces(visit)
+
+
+def units_phase(me, r):
+    arrived(r.S, r.csem2)
+    for lo, hi in ((0, 48), (3072, 3128)):
+        r.E[lo:hi, :] = jnp.zeros((hi - lo, 128), F32)
+
+    def tile(unit, stride, row, lane):
+        r.E[unit_span(unit, stride), :] = r.S[pl.ds(pl.multiple_of(row, 16), 16), lane : lane + 128].astype(F32)
+
+    for_tiles(me, tile)
+
+    def vec(row, unit, count):
+        r.E[unit : unit + count, :] = r.VS[row : row + count, :]
+
+    vec_spots(me, vec)
+    r.tail[...] = r.E[3099:3123, :]
+    up = rdma(r.tail, r.hp, r.hsem2.at[0], r.hsem2.at[1], me.next)
+    down = rdma(r.E.at[0:24], r.hn, r.hsem2.at[2], r.hsem2.at[3], me.prev)
+    up.start()
+    down.start()
+
+    def put(i):
+        r.grad[pl.ds(pl.multiple_of(64 * i, 8), 64), :] = r.E[pl.ds(pl.multiple_of(24 + 64 * i, 8), 64), :]
+
+    loop(48, put)
+    r.grad[3072:3075, :] = r.E[3096:3099, :]
+    up.wait()
+    down.wait()
+    r.grad[0:24, :] += r.hp[...]
+    r.grad[3051:3075, :] += r.hn[...]
+
+
+def whole_layer(me, r):
+    r.VG[...] = jnp.zeros_like(r.VG)
+    r.NB[0] = jnp.zeros((24, 128), F32)
+
+    def clear(slot):
+        r.ZR[slot] = jnp.zeros((1536, 256), BF)
+
+    @pl.when(me.z == 0)
+    def _():
+        loop(4, lambda i: clear(i + 1))
+
+    @pl.when(me.z == 3)
+    def _():
+        loop(4, clear)
+
+    gate(me.quad + me.others + [me.xpeer, me.next, me.prev])
+    prepare(me, r)
+    for s in range(3):
+        gather_step(me, r, s)
+        if s == 0:
+            share_rows(me, r)
+    first_norm(me, r)
+    for s in range(3, 6):
+        gather_step(me, r, s)
+    prepare_drain(me, r)
+    gathered(me, r, (0, 1, 2))
+    attention(me, r, lambda n: gather_step(me, r, 6 + n))
+    gather_step(me, r, 8)
+    gather_step(me, r, 9)
+    gathered(me, r, (3, 4))
+    second_norm(me, r, lambda n: gather_step(me, r, 10 + n))
+    gathered(me, r, (5, 6, 7, 8))
+    hidden(me, r)
+    gathered(me, r, (9, 10, 11))
+    gather_drain(me, r)
+    hidden_grad(me, r)
+    weight_grad(r, r.AC, r.CA, DOWN0, 1024)
+    reduce_send(me, r, (9, 10, 11))
+    weight_grad(r, r.NT, r.GH, UP0, 1024)
+    reduce_send(me, r, (6, 7, 8))
+
+    def steps(*numbers):
+        for s in numbers:
+            reduce_step(me, r, s)
+
+    middle_grad(me, r, lambda n: steps(2 * n, 2 * n + 1))
+    weight_grad(r, r.AT, r.NT, OUT0, 256)
+    reduce_send(me, r, (3, 4, 5))
+    attended_grad(me, r)
+    attention_grad(me, r, lambda n: steps(4))
+    projection_grad(me, r)
+    reduce_send(me, r, (0, 1, 2))
+    steps(5, 6)
+    hidden_sums(me, r)
+    projection_sums(me, r)
+    input_grad(me, r, lambda n: steps(7 + n))
+    for zz in range(4):
+        rdma(r.VG.at[zz * 2 + 1 - me.x], r.VX.at[zz], r.wxs, r.wxr.at[zz], me.xpeer).start()
+    layer_out(me, r, lambda n: steps(9 + n))
+    steps(11, 12, 13)
+    reduce_vectors(me, r)
+    vector_squares(me, r)
+    reduce_last(me, r)
+    norm_exchange(me, r)
+    units_phase(me, r)
+    r.norms[...] = r.NB[5]
+    reduce_drain(me, r)
+    arrived(r.PA.at[0:768], r.asem.at[0])
+    arrived(r.PA.at[0:768], r.asem.at[2])
+
+
+DMA = pltpu.SemaphoreType.DMA
+VMEM = pltpu.VMEM
+SCRATCH = dict(
+    F=VMEM((12288, 256), BF),
+    G=VMEM((12288, 256), BF),
+    XV=VMEM((8, 32, 128), F32),
+    PA=VMEM((1024, 1024), BF),
+    CA=VMEM((1024, 1024), BF),
+    E=VMEM((3128, 128), F32),
+    S=VMEM((1536, 256), BF),
+    VS=VMEM((32, 128), F32),
+    VQ=VMEM((4, 32, 128), F32),
+    VG=VMEM((8, 32, 128), F32),
+    VX=VMEM((4, 32, 128), F32),
+    VZ=VMEM((4, 32, 128), F32),
+    VT=VMEM((4, 32, 128), F32),
+    NB=VMEM((6, 24, 128), F32),
+    NR=VMEM((5, 24, 128), F32),
+    tail=VMEM((24, 128), F32),
+    hp=VMEM((24, 128), F32),
+    hn=VMEM((24, 128), F32),
+    XR=VMEM((4, 1536, 256), BF),
+    ZR=VMEM((5, 1536, 256), BF),
+    QKV=VMEM((3, 1024, 256), BF),
+    P=VMEM((4, 1024, 1024), BF),
+    AT=VMEM((1024, 256), BF),
+    PB=VMEM((1024, 1024), BF),
+    RB=VMEM((5, 256, 1024), BF),
+    MID=VMEM((256, 1024), F32),
+    GMID=VMEM((256, 1024), F32),
+    NT=VMEM((1024, 1024), BF),
+    AC=VMEM((1024, 1024), BF),
+    GP=VMEM((1024, 1024), BF),
+    GH=VMEM((1024, 1024), BF),
+    KV=VMEM((2, 1024, 256), F32),
+    hsem=DMA((4,)), asem=DMA((4,)), qsem=DMA((24,)), csem=DMA, vsem=DMA((2,)), vxs=DMA, vxr=DMA((8,)),
+    xs=DMA, xr=DMA((12,)), zsu=DMA((4,)), zsd=DMA((4,)), zr=DMA((12,)),
+    s1s=DMA((18,)), s1r=DMA((18,)), s2s=DMA((18,)), s2r=DMA((18,)),
+    s3s=DMA((18,)), s3r=DMA((18,)), s4s=DMA((18,)), s4r=DMA((18,)),
+    hsem2=DMA((4,)), rxs=DMA, rxr=DMA((12,)), rzs=DMA((4,)), rzr=DMA((15,)),
+    wxs=DMA, wxr=DMA((4,)), wzs=DMA((4,)), wzr=DMA((4,)), wqs=DMA, wqr=DMA((4,)),
+    qsem2=DMA((96,)), csem2=DMA, nsem=DMA((5,)), nrsem=DMA((5,)),
+)
+
+
+class Refs:
+    pass
+
+
+def fast_layer(lens, pat, cot, par):
+    outs = dict(
+        act=((256, 1024), BF), ing=((256, 1024), BF), grad=((3075, 128), F32), norms=((24, 128), F32)
+    )
+    names = ["lens", "pat", "cot", "par"] + list(outs) + list(SCRATCH)
+
+    def kernel(*refs):
+        r = Refs()
+        for name, ref in zip(names, refs):
+            setattr(r, name, ref)
+        whole_layer(Place(), r)
+
+    whole = pl.BlockSpec(memory_space=pltpu.VMEM)
+    return pl.pallas_call(
+        kernel,
+        out_shape=[jax.ShapeDtypeStruct(*o) for o in outs.values()],
+        in_specs=[pl.BlockSpec(memory_space=pltpu.SMEM)] + [whole] * 3,
+        out_specs=[whole] * len(outs),
+        scratch_shapes=list(SCRATCH.values()),
+        compiler_params=pltpu.CompilerParams(collective_id=0, has_side_effects=True, vmem_limit_bytes=VMEM_LIMIT),
+    )(lens, pat, cot, par)
+
+
+VMEM_LIMIT = 63 * 2**20
+PLAIN_UNITS = ((0, 16), (24592, 24608), (32800, 32824), (65592, 65624), (98392, 98400))
+
+
+def fast_shards(pat, cot, lens, params, m, v):
+    def units(a):
+        return a.reshape(-1, LANE)
+
+    par = units(params)
+    act, ing, grad, nb = fast_layer(lens[0], pat[0], cot[0], par)
+    norms = jnp.sum(nb[:GROUPS], axis=1)
+    clip = 1.0 / jnp.maximum(jnp.sqrt(jnp.sum(norms)), 1.0)
+    start = lax.axis_index(("dp", "blk")) * par.shape[0]
+    unit = start + lax.broadcasted_iota(jnp.int32, par.shape, 0)
+    plain = jnp.zeros(par.shape, jnp.bool_)
+    for lo, hi in PLAIN_UNITS:
+        plain = plain | ((unit >= lo) & (unit < hi))
+    scaled = clip * grad
+    first = 0.9 * units(m) + 0.1 * scaled
+    second = 0.999 * units(v) + 0.001 * scaled * scaled
+    direction = first / (1.0 - 0.9**10) / (jnp.sqrt(second / (1.0 - 0.999**10)) + 1e-08)
+    step = -0.001 * 0.9**12 * (direction + jnp.where(plain, 0.0, 0.05 * par))
+    return act[None], ing[None], norms, step.reshape(-1), first.reshape(-1), nb[16:24].reshape(-1)
+
+
 def solution(mesh):
-    in_specs = (
-        P("dp", "blk", None),
-        P("dp", "blk", None),
-        P("dp", None),
-        P(("dp", "blk")),
-        P(("dp", "blk")),
-        P(("dp", "blk")),
-    )
-    out_specs = (
-        P("dp", "blk", None),
-        P("dp", "blk", None),
-        P(),
-        P(("dp", "blk")),
-        P(("dp", "blk")),
-        P(),
-    )
-    return jax.shard_map(shards, mesh=mesh, in_specs=in_specs, out_specs=out_specs, check_vma=False)
+    act, flat = P("dp", "blk", None), P(("dp", "blk"))
+    specs = dict(
+        in_specs=(act, act, P("dp", None), flat, flat, flat), out_specs=(act, act, P(), flat, flat, P()), check_vma=False
+    )
+
+    def layer(patches, cotangent, image_lengths, params, first_moment, second_moment):
+        fits = (dict(mesh.shape), patches.shape, params.shape) == (dict(dp=8, blk=4), (8, 1024, D), (RAW,))
+        step = jax.shard_map(fast_shards if fits else shards, mesh=mesh, **specs)
+        return step(patches, cotangent, image_lengths, params, first_moment, second_moment)
+
+    return layer

time: 1640 us -> 292 us (0.18)
  waiting for transfers between devices: 991 us -> 0 us
  Pallas kernels: 0 us -> 281 us
  local copies, waits for them, and re-layouts: 252 us -> 2.87 us
  other arithmetic: 216 us -> 6.33 us
  matrix products: 117 us -> 0 us
  blocking collectives: 40 us -> 0 us
    unnamed x5 -> x0, waiting for transfers between devices: 696 us -> none
    pallas_call x0 -> x1, Pallas kernels: none -> 281 us  [fast_layer(): pl.pallas_call(kernel, out_shape=[jax.ShapeDtypeStruct(*o) for o in outs....]
    all_gather x2 -> x0, waiting for transfers between devices: 278 us -> none  [the longest x1 278 us: shards(): lax.all_gather(params.astype(jnp.bfloat16), ('dp', 'blk'), axis=0, tiled=...]
    unnamed x120 -> x6, local copies, waits for them, and re-layouts: 153 us -> 1.59 us
    all_gather x1 -> x0, other arithmetic: 149 us -> none  [shards(): lax.all_gather(params.astype(jnp.bfloat16), ('dp', 'blk'), axis=0, tiled=...]
    dot_general x26 -> x0, matrix products: 117 us -> none  [the longest x1 16.7 us: shards(): jnp.dot(normed_two_low, w_up, preferred_element_type=jnp.float32)]
    reduce_sum x16 -> x1, other arithmetic: 51.1 us -> 1.33 us  [fast_shards(): clip = 1.0 / jnp.maximum(jnp.sqrt(jnp.sum(norms)), 1.0)]
    psum x1 -> x0, blocking collectives: 40 us -> none  [shards(): norms, bias_total = lax.psum((partials, grad_bias_down), ('dp', 'blk'))]
  transfers between devices with their start and end apart: 4 -> 0, of which waited for: 3 -> 0; matrix products, arithmetic and copies ran while one was open for 6% -> 0% of each run, Pallas kernels for 0% -> 0%
where the time goes in v2:
time: 292 us
  Pallas kernels  281 us (96%)
  other arithmetic  6.33 us (2%)
    pallas_call x1, Pallas kernels, fast_layer(): pl.pallas_call(kernel, out_shape=[jax.ShapeDtypeStruct(*o) for o in outs....  281 us

profile of v2, /device:TPU:0, one launch (start us, length us, event | category | flops | bytes accessed | tf_op | source)
XLA Modules:
  0.0 291.9 jit_solution(9218713633690959012)
XLA Ops:
  0.7 281.3 %shard_map.109 = (bf16[256,1024]{1,0:T(8,128)(2,1)}, bf16[256,1024]{1,0:T(8,128)(2,1)}, f32[3075,128]{1,0:T(8,128)}, f32[24,128]{1,0:T(8,128)}) custom-call(s32[9]{0:T(128)} %bitcast.28, bf16[256,1024]{1,0:T(8,128)(2,1)} %bitcast.26, bf16[256,1024]{1,0:T(8,128)(2,1)} %bitcast.27, f32[3075,128]{1,0:T(8,128)} %bitcast.23), custom_call_target="tpu_custom_call" | custom-call | tf_op jit(solution)/shard_map/pallas_call | solution.py:1346
  282.0 1.3 slice_reduce_fusion
  284.1 1.3 slice_bitcast_fusion
  285.4 0.0 copy-start.1
  285.4 0.0 copy-start
  285.4 5.0 %fusion.6 = (f32[393600]{0:T(1024)}, f32[393600]{0:T(1024)}) fusion(f32[3075,128]{1,0:T(8,128)} %get-tuple-element.13, f32[393600]{0:T(1024)} %param.10, f32[]{:T(128)S(6)} %div.18, f32[393600]{0:T(1024)} %param.9, pred[3075]{0:T(1024)(128)(4,1)S(1)} %fusion.21, f32[393600]{0:T(1024)} %param.11), kind=kLoop, calls=%fused_computation.9 | loop fusion | flops 6297600 | bytes 9449479 | tf_op jit(solution)/shard_map/reshape | solution.py:1378
  290.3 0.0 copy-done.1
  290.3 0.8 copy.14
  291.1 0.0 copy-done
  291.1 0.8 copy.15
  (1 shorter events, 0.0 us)
Async XLA Ops:
  285.4 5.0 %copy-start.1 = (bf16[256,1024]{1,0:T(8,128)(2,1)S(1)}, bf16[256,1024]{1,0:T(8,128)(2,1)}, u32[]{:S(2)}) copy-start(bf16[256,1024]{1,0:T(8,128)(2,1)} %get-tuple-element.10) | copy-start | bytes 1572868
  285.4 5.8 %copy-start = (bf16[256,1024]{1,0:T(8,128)(2,1)S(1)}, bf16[256,1024]{1,0:T(8,128)(2,1)}, u32[]{:S(2)}) copy-start(bf16[256,1024]{1,0:T(8,128)(2,1)} %get-tuple-element.11) | copy-start | bytes 1572868
